TPU v7x, 256 devices: a whole 4x4x8 slice. The times are simulated.
256 devices in a mesh: dp: 4 (over x), ctx: 64 (over z, y, core).
Axes of the slice: x: 4, y: 4, z: 8, core: 2. Of those that a mesh axis runs over, the one named last changes fastest.
Arguments:
- raw_qkv: bfloat16 [4, 3, 4096, 10240], P('dp', None, None, 'ctx'), may hold values from -6 to 6
- block_lengths: int32 [4, 64, 2], P('dp', 'ctx'), may hold values from 1 to 159, as said below
- short_filter: float32 [3, 256, 7], replicated, may hold values from -2 to 2
- medium_filter: float32 [256, 64], replicated, may hold values from -0.75 to 0.75
- doc_span: int32 [4, 2, 8192], P('dp', None, 'ctx'), may hold values from 0 to 285, as said below
- cotangent: bfloat16 [4, 4096, 8192], P('dp', None, 'ctx'), may hold values from -6 to 6
Outputs:
- grad_qkv: bfloat16 [4, 3, 4096, 8192], P('dp', None, None, 'ctx')
- grad_short: float32 [3, 256, 7], replicated
- grad_medium: float32 [256, 64], replicated
Inputs may be any that keep to these rules, and one draw needn't show every extreme that they name: Entry k of block_lengths[n, i] is the length of the k-th document piece among the live rows of block i, which are its first live[n, i] rows. The first piece of every block but block 0 continues the document that ends the block before. start[n, i] differs from i * 128 by at most 16; in every sequence some block starts 16 rows late and another 16 rows early. All blocks of a sequence together hold 8192 live rows. `doc_span`: row 0 counts the tokens of the same document before a packed token, row 1 those after it, for the documents that block_lengths describes.
All inputs are finite; a program needn't handle non-finite values.
Results may differ from a plain program's by a relative error of at most 0.008.
Values may be sent and summed in bfloat16 or wider, within the bound.
A program may use at most 192 MiB of HBM per device.

v0:
```python
import math

import jax
import jax.numpy as jnp
from jax import lax
from jax.sharding import PartitionSpec as P


def entering(part, axis, combine, identity):
    place = lax.axis_index(axis)
    gathered = lax.all_gather(part, axis)
    state = jnp.zeros_like(part) + jnp.asarray(identity, part.dtype)

    def one(lap, state):
        return combine(state, lax.dynamic_index_in_dim(gathered, lap, 0, False))

    return lax.fori_loop(0, place, one, state)


def with_halo(block, sides, width):
    for axis, dim in sides:
        count = lax.axis_size(axis)
        forward = [(i, i + 1) for i in range(count - 1)]
        backward = [(target, source) for source, target in forward]
        low = lax.ppermute(
            lax.slice_in_dim(block, block.shape[dim] - width, None, axis=dim), axis, forward
        )
        high = lax.ppermute(lax.slice_in_dim(block, 0, width, axis=dim), axis, backward)
        block = jnp.concatenate([low, block, high], axis=dim)
    return block


def passed_along(block, axis, distance):
    devices = range(lax.axis_size(axis))
    route = [(i - distance, i) for i in devices if i - distance in devices]
    return lax.ppermute(block, axis, route)


def add_counts(earlier, later):
    return earlier + later


def skewed(pattern, row_count, col_count):
    lead_shape = pattern.shape[:-1]
    tiled = jnp.tile(pattern, (1,) * len(lead_shape) + (row_count,))
    return tiled[..., : row_count * col_count].reshape(lead_shape + (row_count, col_count))


def short_pass(source, short_wide, before, count):
    tap_count = short_wide.shape[2]
    summed = jnp.zeros((source.shape[0], source.shape[1], count), jnp.float32)
    for tap_lag in range(tap_count):
        window = source[:, :, tap_count - 1 - tap_lag : tap_count - 1 - tap_lag + count].astype(
            jnp.float32
        )
        factor = short_wide[:, :, tap_lag : tap_lag + 1].astype(jnp.float32)
        summed = summed + jnp.where(tap_lag <= before, factor * window, 0.0)
    return summed


def edge_columns(raw_rows, live_rows, reach_rows):
    capacity = raw_rows.shape[3]
    head_cols = raw_rows[:, :, :, :reach_rows]
    picks = jnp.clip(
        live_rows - reach_rows + jnp.arange(reach_rows, dtype=jnp.int32), 0, capacity - 1
    )
    tail_cols = jnp.take(raw_rows, picks, axis=3)
    return jnp.concatenate([head_cols, tail_cols], axis=3)


def forward_bands(medium_bf, before, row_count):
    group_total, tap_count = medium_bf.shape
    col_count = row_count + tap_count - 1
    group_block = math.gcd(group_total, 32)
    out_index = jnp.arange(row_count, dtype=jnp.int32)[:, None]
    in_index = jnp.arange(col_count, dtype=jnp.int32)[None, :]
    allowed = out_index + tap_count - 1 - in_index <= before[:, None]

    def build(subset):
        filler = jnp.zeros((subset.shape[0], row_count), subset.dtype)
        pattern = jnp.concatenate([subset[:, ::-1], filler], axis=1)
        return jnp.where(
            allowed[None], skewed(pattern, row_count, col_count), jnp.zeros((), subset.dtype)
        )

    stacked = lax.map(build, medium_bf.reshape(group_total // group_block, group_block, tap_count))
    return stacked.reshape(group_total, row_count, col_count)


def medium_taps_grad(weighted_groups, mixed_groups, before, tap_count):
    group_total, group_size, row_count = weighted_groups.shape
    span_cols = 2 * tap_count - 1
    tap_lag = tap_count - 1 - jnp.arange(tap_count, dtype=jnp.int32)

    def block_out(number):
        first = number * tap_count
        left_op = lax.dynamic_slice_in_dim(weighted_groups, first, tap_count, 2)
        right_op = lax.dynamic_slice_in_dim(mixed_groups, first, span_cols, 2)
        local_before = lax.dynamic_slice_in_dim(before, first, tap_count, 0)
        product = jnp.einsum("gct,gcu->gtu", left_op, right_op, preferred_element_type=jnp.float32)
        flattened = jnp.pad(product, ((0, 0), (0, 0), (0, 1))).reshape(
            group_total, tap_count * 2 * tap_count
        )
        flattened = jnp.pad(flattened, ((0, 0), (0, tap_count)))
        diagonal = flattened.reshape(group_total, tap_count, 2 * tap_count + 1)[:, :, :tap_count]
        allowed = tap_lag[None, :] <= local_before[:, None]
        return jnp.sum(jnp.where(allowed[None], diagonal, 0.0), axis=1)[:, ::-1]

    parts = lax.map(block_out, jnp.arange(row_count // tap_count, dtype=jnp.int32))
    return jnp.sum(parts, axis=0)


def shards(raw_qkv, block_lengths, short_filter, medium_filter, doc_span, cotangent):
    row_count = cotangent.shape[2]
    channels = cotangent.shape[1]
    capacity = raw_qkv.shape[3]
    drift_rows = (capacity - row_count) // 2
    group_total, tap_count = medium_filter.shape
    group_size = channels // group_total
    short_count = short_filter.shape[2]
    head_cols = short_count - 1
    history_rows = short_count + tap_count - 2
    device_index = lax.axis_index("ctx")
    live_rows = jnp.sum(block_lengths)
    start_row = entering(live_rows, "ctx", add_counts, jnp.zeros((), jnp.int32))
    beside_all = with_halo(edge_columns(raw_qkv, live_rows, drift_rows), (("ctx", 3),), drift_rows)
    source = jnp.concatenate(
        [beside_all[:, :, :, :drift_rows], raw_qkv, beside_all[:, :, :, 3 * drift_rows :]], axis=3
    )
    offset = device_index * row_count + jnp.arange(row_count, dtype=jnp.int32) - start_row
    column = jnp.where(
        offset < live_rows, drift_rows + offset, drift_rows + capacity + offset - live_rows
    )
    packed = jnp.take(source, column, axis=3)[0]
    before = doc_span[0, 0]
    following = doc_span[0, 1]
    short_wide = jnp.repeat(short_filter.astype(jnp.bfloat16), group_size, axis=1)
    medium_bf = medium_filter.astype(jnp.bfloat16)
    recent = short_pass(
        packed[:, :, row_count - history_rows :],
        short_wide,
        before[row_count - tap_count + 1 :],
        tap_count - 1,
    )
    recent_mixed = (recent[1] * recent[2]).astype(jnp.bfloat16)
    last_inputs = jnp.transpose(packed[:, :, row_count - head_cols :], (1, 0, 2)).reshape(
        channels, 3 * head_cols
    )
    incoming = passed_along(jnp.concatenate([recent_mixed, last_inputs], axis=1), "ctx", 1)
    prior_inputs = jnp.transpose(
        incoming[:, tap_count - 1 :].reshape(channels, 3, head_cols), (1, 0, 2)
    )
    inputs_ext = jnp.concatenate([prior_inputs, packed], axis=2)
    filtered = short_pass(inputs_ext, short_wide, before, row_count)
    mixed_ext = jnp.concatenate(
        [incoming[:, : tap_count - 1], (filtered[1] * filtered[2]).astype(jnp.bfloat16)], axis=1
    )
    bands = forward_bands(medium_bf, before, row_count)
    mixed_groups = mixed_ext.reshape(group_total, group_size, row_count + tap_count - 1)
    response = jnp.einsum(
        "gcu,gtu->gct", mixed_groups, bands, preferred_element_type=jnp.float32
    ).reshape(channels, row_count)
    upstream = cotangent[0].astype(jnp.float32)
    weighted = (upstream * filtered[0]).astype(jnp.bfloat16)
    grad_query = upstream * response
    weighted_groups = weighted.reshape(group_total, group_size, row_count)
    spread_all = jnp.einsum(
        "gct,gtu->gcu", weighted_groups, bands, preferred_element_type=jnp.float32
    )
    spread = spread_all.reshape(channels, row_count + tap_count - 1)[:, tap_count - 1 :]
    grad_head = jnp.stack(
        [
            grad_query[:, :head_cols],
            spread[:, :head_cols] * filtered[2][:, :head_cols],
            spread[:, :head_cols] * filtered[1][:, :head_cols],
        ]
    ).astype(jnp.bfloat16)
    outgoing_back = jnp.concatenate(
        [
            weighted[:, : tap_count - 1],
            jnp.transpose(grad_head, (1, 0, 2)).reshape(channels, 3 * head_cols),
        ],
        axis=1,
    )
    incoming_back = passed_along(outgoing_back, "ctx", -1)
    later_weighted = incoming_back[:, : tap_count - 1].reshape(
        group_total, group_size, tap_count - 1
    )
    later_grad = jnp.transpose(
        incoming_back[:, tap_count - 1 :].reshape(channels, 3, head_cols), (1, 0, 2)
    )
    own_index = jnp.arange(tap_count - 1, dtype=jnp.int32)[:, None]
    next_index = jnp.arange(tap_count - 1, dtype=jnp.int32)[None, :]
    tail_following = following[row_count - tap_count + 1 :]
    allowed = (next_index <= own_index) & (
        tap_count - 1 + next_index - own_index <= tail_following[:, None]
    )
    coupling = jnp.where(
        allowed[None],
        skewed(jnp.roll(medium_bf, 1, axis=1), tap_count - 1, tap_count - 1),
        jnp.zeros((), jnp.bfloat16),
    )
    incoming_terms = jnp.einsum(
        "gct,gst->gcs", later_weighted, coupling, preferred_element_type=jnp.float32
    ).reshape(channels, tap_count - 1)
    spread = jnp.concatenate(
        [
            spread[:, : row_count - tap_count + 1],
            spread[:, row_count - tap_count + 1 :] + incoming_terms,
        ],
        axis=1,
    )
    grad_filtered = jnp.stack([grad_query, spread * filtered[2], spread * filtered[1]]).astype(
        jnp.bfloat16
    )
    grad_ext = jnp.concatenate([grad_filtered, later_grad], axis=2)
    grad_inputs = jnp.zeros((3, channels, row_count), jnp.float32)
    short_terms = []
    for tap_lag in range(short_count):
        factor = short_wide[:, :, tap_lag : tap_lag + 1].astype(jnp.float32)
        ahead = grad_ext[:, :, tap_lag : tap_lag + row_count].astype(jnp.float32)
        grad_inputs = grad_inputs + jnp.where(tap_lag <= following, factor * ahead, 0.0)
        behind = inputs_ext[
            :, :, short_count - 1 - tap_lag : short_count - 1 - tap_lag + row_count
        ].astype(jnp.float32)
        per_channel = jnp.sum(
            jnp.where(tap_lag <= before, grad_filtered.astype(jnp.float32) * behind, 0.0), axis=2
        )
        short_terms.append(jnp.sum(per_channel.reshape(3, group_total, group_size), axis=2))
    short_grad = jnp.stack(short_terms, axis=2)
    medium_grad = medium_taps_grad(weighted_groups, mixed_groups, before, tap_count)
    short_sum, medium_sum = lax.psum((short_grad, medium_grad), ("dp", "ctx"))
    scale = math.sqrt(lax.axis_size("dp") * lax.axis_size("ctx") * row_count * group_size)
    return (grad_inputs.astype(jnp.bfloat16)[None], short_sum / scale, medium_sum / scale)


def solution(mesh):
    return jax.shard_map(
        shards,
        mesh=mesh,
        in_specs=(
            P("dp", None, None, "ctx"),
            P("dp", "ctx", None),
            P(),
            P(),
            P("dp", None, "ctx"),
            P("dp", None, "ctx"),
        ),
        out_specs=(P("dp", None, None, "ctx"), P(), P()),
        check_vma=False,
    )
```

profile of v0, /device:TPU:1, one launch (start us, length us, event | category | flops | bytes accessed | tf_op | source)
XLA Modules:
  0.0 928.6 jit_solution(12846568738952805797)
XLA Ops:
  31.0 19.7 %all-reduce.3 = s32[64]{0:T(128)S(1)} all-reduce(s32[64]{0:T(128)S(1)} %dynamic-update-slice), channel_id=1, replica_groups=mesh['dp'=4,'ctx'=64] {'ctx'}, use_global_device_ids=true, to_apply=%add.3 | all-reduce | flops 64 | bytes 512
  59.5 131.8 %while.35 = (s32[]{:T(128)}, bf16[8,32,128,191]{3,2,1,0:T(8,128)(2,1)}, bf16[8,32,64]{2,1,0:T(8,128)(2,1)}, s32[128]{0:T(128)S(1)}, s32[128]{0:T(128)S(1)}, /*index=5*/s32[]{:T(128)}, bf16[]{:T(256)}) while((s32[]{:T(128)}, bf16[8,32,128,191]{3,2,1,0:T(8,128)(2,1)}, bf16[8,32,64]{2,1,0:T(8,128)(2,1)}, s32[128]{0:T(128)S(1)}, ...), condition=%wide.region_4.5_spmd.clone, body=%wide.region_3.4_spmd.clone.sunk | while | flops 831234 | bytes 14734175 | solution.py:86
  66.4 7.7 reshape.371
  82.9 7.7 reshape.371
  99.4 7.7 reshape.371
  115.8 7.7 reshape.371
  132.3 7.7 reshape.371
  148.7 7.7 reshape.371
  165.2 7.7 reshape.371
  181.6 7.7 reshape.371
  197.9 8.2 copy.246
  210.0 11.1 %maximum_bitcast_fusion = bf16[3,4096,192]{1,0,2:T(4,128)(2,1)} fusion(bf16[1,3,4096,16]{2,1,3,0:T(4,128)(2,1)S(1)} %collective-permute-done.1, bf16[1,3,4096,160]{2,1,3,0:T(4,128)(2,1)} %copy-done.4, bf16[1,3,4096,16]{2,1,3,0:T(4,128)(2,1)S(1)} %collective-permute-done), kind=kLoop, calls=%fused_computation.76 | loop fusion | flops 4718592 | bytes 9437184 | tf_op jit(solution)/shard_map/concatenate | solution.py:127
  221.0 10.5 %gather_fusion.1 = bf16[128,3,4096]{2,1,0:T(4,128)(2,1)} fusion(bf16[3,4096,192]{1,0,2:T(4,128)(2,1)} %maximum_bitcast_fusion, s32[1024]{0:T(1024)S(1)} %pad_clamp_fusion), kind=kCustom, calls=%fused_computation.1 | custom fusion | bytes 6291968 | tf_op jit(solution)/shard_map/jit(_take)/gather | solution.py:134
  231.6 7.4 copy.231
  251.7 18.7 %select_add_fusion = f32[3,4096,63]{2,1,0:T(8,128)S(1)} fusion(bf16[3,4096,128]{2,1,0:T(8,128)(2,1)S(1)} %select_bitcast_fusion, f32[3,4096]{1,0:T(4,128)S(1)} %get-tuple-element.265, f32[3,4096]{1,0:T(4,128)S(1)} %get-tuple-element.266, f32[3,4096]{1,0:T(4,128)S(1)} %get-tuple-element.267, f32[3,4096]{1,0:T(4,128)S(1)} %get-tuple-element.268, ...), kind=kLoop, calls=%fused_computation.78 | loop fusion | flops 20901888 | bytes 14279097 | tf_op jit(solution)/shard_map/add | solution.py:57
  274.5 6.6 collective-permute-start.2
  296.8 26.4 %fusion.15 = f32[3,4096,128]{2,1,0:T(8,128)S(1)} fusion(bf16[3,4096,128]{2,1,0:T(8,128)(2,1)S(1)} %select_bitcast_fusion, f32[3,4096]{1,0:T(4,128)S(1)} %get-tuple-element.265, f32[3,4096]{1,0:T(4,128)S(1)} %get-tuple-element.266, f32[3,4096]{1,0:T(4,128)S(1)} %get-tuple-element.267, f32[3,4096]{1,0:T(4,128)S(1)} %get-tuple-element.268, ...), kind=kLoop, calls=%fused_computation.47 | loop fusion | flops 70778880 | bytes 9929600 | tf_op jit(solution)/shard_map/add | solution.py:57
  330.3 11.6 %fusion.65 = f32[256,16,128]{2,1,0:T(8,128)} fusion(bf16[256,16,191]{2,1,0:T(8,128)(2,1)S(1)} %bitcast.186, bf16[256,128,191]{2,1,0:T(8,128)(2,1)} %bitcast.177), kind=kOutput, calls=%fused_computation.189 | convolution fusion | flops 200278016 | bytes 16179200 | tf_op jit(solution)/shard_map/gcu,gtu->gct/dot_general | solution.py:160
  341.9 6.1 slice_bitcast_fusion.2
  348.0 7.0 fusion.66
  378.3 73.3 %while.36 = (s32[]{:T(128)}, f32[2,256,64]{1,2,0:T(8,128)S(1)}, s32[2]{0:T(128)S(1)}, s32[128]{0:T(128)S(1)}, bf16[256,16,128]{2,1,0:T(8,128)(2,1)S(1)}, /*index...) while((s32[]{:T(128)}, f32[2,256,64]{1,2,0:T(8,128)S(1)}, ...), condition=%wide.region_22.23_spmd.clone, body=%wide.region_20.22_spmd.clone.sunk | while | flops 68669512 | bytes 82060776 | solution.py:109
  379.8 6.3 fusion.80
  386.1 9.3 %copy.276 = f32[256,64,127]{0,2,1:T(8,128)} copy(f32[256,64,127]{2,1,0:T(8,128)} %fusion.80) | data formatting | bytes 16646144 | tf_op jit(solution)/shard_map/while
  402.9 9.3 reshape.372
  416.3 6.3 fusion.80
  422.6 9.3 %copy.276 = f32[256,64,127]{0,2,1:T(8,128)} copy(f32[256,64,127]{2,1,0:T(8,128)} %fusion.80) | data formatting | bytes 16646144 | tf_op jit(solution)/shard_map/while
  439.4 9.3 reshape.372
  455.9 302.2 %all-reduce.6.cloned.1.call-done = f32[256,64]{1,0:T(8,128)} async-done(((f32[256,64]{1,0:T(8,128)}), f32[256,64]{1,0:T(8,128)}) %all-reduce.6.cloned.1.call-update) | async-done | bytes 65552 | tf_op jit(solution)/shard_map/psum | solution.py:232
  770.8 13.2 %fusion.39 = (f32[3,4096]{1,0:T(4,128)}, f32[3,4096]{1,0:T(4,128)}, f32[3,4096]{1,0:T(4,128)}, f32[3,4096]{1,0:T(4,128)}) fusion(pred[128]{0:T(512)(128)(4,1)S(1)} %copy-done.31, bf16[3,4096,128]{2,1,0:T(8,128)(2,1)S(1)} %copy-done.1, bf16[3,4096,6]{2,1,0:T(8,128)(2,1)S(1)} %bitcast.184, bf16[1,4096,128]{2,1,0:T(8,128)(2,1)S(1)} %get-tuple-element.226, ...), kind=kLoop, calls=%fused_computation.71 | loop fusion | flops 48709632 | bytes 6636032 | tf_op jit(solution)/shard_map/reduce_sum | solution.py:226
  784.1 10.5 %fusion.43 = (f32[3,4096]{1,0:T(4,128)}, f32[3,4096]{1,0:T(4,128)}, f32[3,4096]{1,0:T(4,128)}) fusion(pred[128]{0:T(512)(128)(4,1)S(1)} %copy-done.26, bf16[3,4096,128]{2,1,0:T(8,128)(2,1)S(1)} %copy-done.1, bf16[3,4096,6]{2,1,0:T(8,128)(2,1)S(1)} %bitcast.185, bf16[1,4096,128]{2,1,0:T(8,128)(2,1)S(1)} %get-tuple-element.226, ...), kind=kLoop, calls=%fused_computation.75 | loop fusion | flops 42430464 | bytes 6586752 | tf_op jit(solution)/shard_map/reduce_sum | solution.py:226
  818.9 76.4 %psum.14 = f32[3,256,7]{1,0,2:T(4,128)S(1)} all-reduce(f32[3,256,7]{1,0,2:T(4,128)} %constant_dynamic-update-slice_fusion), channel_id=1, replica_groups=mesh['dp'=4,'ctx'=64] {'dp','ctx'}, use_global_device_ids=true, to_apply=%region_19.20 | all-reduce | flops 5376 | bytes 43008 | tf_op jit(solution)/shard_map/psum | solution.py:232
  895.9 25.3 %fusion.49 = bf16[1,3,4096,128]{3,2,1,0:T(8,128)(2,1)} fusion(bf16[3,4096,134]{2,1,0:T(8,128)(2,1)} %pad_maximum_fusion, f32[3,4096]{1,0:T(4,128)} %copy-done.11, pred[128]{0:T(512)(128)(4,1)} %get-tuple-element.250, f32[3,4096]{1,0:T(4,128)} %copy-done.12, pred[128]{0:T(512)(128)(4,1)} %get-tuple-element.249, f32[3,4096]{1,0:T(4,128)} %copy-done.13, ...), kind=kLoop, calls=%fused_computation.91 | loop fusion | flops 47185920 | bytes 25510784 | tf_op jit(solution)/shard_map/broadcast_in_dim | solution.py:234
  (280 shorter events, 239.3 us)
Async XLA Ops:
  7.2 14.1 %copy-start.36 = (s32[1,1,2]{2,1,0:T(1,128)S(1)}, s32[1,1,2]{2,1,0:T(1,128)}, u32[]{:S(2)}) copy-start(s32[1,1,2]{2,1,0:T(1,128)} %param.13) | copy-start | bytes 28
  7.2 750.9 %all-reduce.6.cloned.1.call-start = ((), (), s32[]{:S(2)}) async-start(), calls=%async_computation | async-start | bytes 262144 | tf_op jit(solution)/shard_map/psum | solution.py:232
  15.0 14.0 %copy-start.37 = (u32[256]{0:T(256)S(1)}, u32[256]{0:T(256)}, u32[]{:S(2)}) copy-start(u32[256]{0:T(256)} %constant.155) | copy-start | bytes 3076
  15.0 39.2 %copy-start.32 = (s32[1,2,128]{2,1,0:T(2,128)S(1)}, s32[1,2,128]{2,1,0:T(2,128)}, u32[]{:S(2)}) copy-start(s32[1,2,128]{2,1,0:T(2,128)} %param.16) | copy-start | bytes 3076
  15.0 39.8 %copy-start.17 = (f32[256,64]{0,1:T(8,128)S(1)}, f32[256,64]{0,1:T(8,128)}, u32[]{:S(2)}) copy-start(f32[256,64]{0,1:T(8,128)} %param.15) | copy-start | bytes 196612
  15.1 40.6 %copy-start.18 = (f32[3,256,7]{1,2,0:T(8,128)S(1)}, f32[3,256,7]{1,2,0:T(8,128)}, u32[]{:S(2)}) copy-start(f32[3,256,7]{1,2,0:T(8,128)} %param.14) | copy-start | bytes 64516
  16.1 193.9 %collective-permute-start.1 = (bf16[1,3,4096,16]{2,1,3,0:T(4,128)(2,1)}, bf16[1,3,4096,16]{2,1,3,0:T(4,128)(2,1)S(1)}, u32[]{:S(2)}, u32[]{:S(2)}) collective-permute-start(bf16[1,3,4096,16]{2,1,3,0:T(4,128)(2,1)} %slice.266), channel_id=1, source_target_pairs={{1,0},{2,1},{3,2},{4,3},{5,4},{6,5},{7,6},{8,7},{9,8},{10,9},{11,1... | collective-permute-start | bytes 1179656 | tf_op jit(solution)/shard_map/ppermute | solution.py:28
  27.2 182.8 %collective-permute-start = (bf16[1,3,4096,16]{2,1,3,0:T(4,128)(2,1)}, bf16[1,3,4096,16]{2,1,3,0:T(4,128)(2,1)S(1)}, u32[]{:S(2)}, u32[]{:S(2)}) collective-permute-start(bf16[1,3,4096,16]{2,1,3,0:T(4,128)(2,1)} %bitcast_select_fusion), channel_id=1, source_target_pairs={{0,1},{1,2},{2,3},{3,4},{4,5},{5,6},{6,7},{7,8},{8,9},{9,10},{10,1... | collective-permute-start | bytes 1179656 | tf_op jit(solution)/shard_map/ppermute | solution.py:25
  54.8 241.9 %copy-start.21 = (pred[128]{0:T(512)(128)(4,1)}, pred[128]{0:T(512)(128)(4,1)S(1)}, u32[]{:S(2)}) copy-start(pred[128]{0:T(512)(128)(4,1)S(1)} %get-tuple-element.259) | copy-start | bytes 388
  54.8 241.9 %copy-start.23 = (pred[128]{0:T(512)(128)(4,1)}, pred[128]{0:T(512)(128)(4,1)S(1)}, u32[]{:S(2)}) copy-start(pred[128]{0:T(512)(128)(4,1)S(1)} %get-tuple-element.263) | copy-start | bytes 388
  54.8 241.9 %copy-start.25 = (pred[128]{0:T(512)(128)(4,1)}, pred[128]{0:T(512)(128)(4,1)S(1)}, u32[]{:S(2)}) copy-start(pred[128]{0:T(512)(128)(4,1)S(1)} %get-tuple-element.264) | copy-start | bytes 388
  59.5 237.2 %copy-start.10 = (f32[3,4096,1]{1,0,2:T(4,128)}, f32[3,4096,1]{1,0,2:T(4,128)S(1)}, u32[]{:S(2)}) copy-start(f32[3,4096,1]{1,0,2:T(4,128)S(1)} %copy.273) | copy-start | bytes 147460
  196.1 12.6 %copy-start.33 = (s32[1,2,128]{2,1,0:T(2,128)S(1)}, s32[1,2,128]{2,1,0:T(2,128)}, u32[]{:S(2)}) copy-start(s32[1,2,128]{2,1,0:T(2,128)} %param.16) | copy-start | bytes 3076
  206.1 90.5 %copy-start.11 = (f32[3,4096]{1,0:T(4,128)}, f32[3,4096]{1,0:T(4,128)S(1)}, u32[]{:S(2)}) copy-start(f32[3,4096]{1,0:T(4,128)S(1)} %get-tuple-element.265) | copy-start | bytes 147460
  206.2 90.5 %copy-start.12 = (f32[3,4096]{1,0:T(4,128)}, f32[3,4096]{1,0:T(4,128)S(1)}, u32[]{:S(2)}) copy-start(f32[3,4096]{1,0:T(4,128)S(1)} %get-tuple-element.266) | copy-start | bytes 147460
  207.1 89.6 %copy-start.13 = (f32[3,4096]{1,0:T(4,128)}, f32[3,4096]{1,0:T(4,128)S(1)}, u32[]{:S(2)}) copy-start(f32[3,4096]{1,0:T(4,128)S(1)} %get-tuple-element.267) | copy-start | bytes 147460
  207.1 89.6 %copy-start.14 = (f32[3,4096]{1,0:T(4,128)}, f32[3,4096]{1,0:T(4,128)S(1)}, u32[]{:S(2)}) copy-start(f32[3,4096]{1,0:T(4,128)S(1)} %get-tuple-element.268) | copy-start | bytes 147460
  208.7 88.1 %copy-start.15 = (f32[3,4096]{1,0:T(4,128)}, f32[3,4096]{1,0:T(4,128)S(1)}, u32[]{:S(2)}) copy-start(f32[3,4096]{1,0:T(4,128)S(1)} %get-tuple-element.269) | copy-start | bytes 147460
  231.6 7.4 copy-start.34
  241.1 55.6 %copy-start = (bf16[3,4096,128]{2,1,0:T(8,128)(2,1)}, bf16[3,4096,128]{2,1,0:T(8,128)(2,1)S(1)}, u32[]{:S(2)}) copy-start(bf16[3,4096,128]{2,1,0:T(8,128)(2,1)S(1)} %select_bitcast_fusion) | copy-start | bytes 9437188
  241.1 10.6 %copy-start.35 = (pred[63]{0:T(512)(128)(4,1)S(1)}, pred[63]{0:T(512)(128)(4,1)}, u32[]{:S(2)}) copy-start(pred[63]{0:T(512)(128)(4,1)} %get-tuple-element.251) | copy-start | bytes 193
  251.7 18.9 %copy-start.8 = (bf16[4096,18]{1,0:T(8,128)(2,1)S(1)}, bf16[4096,18]{1,0:T(8,128)(2,1)}, u32[]{:S(2)}) copy-start(bf16[4096,18]{1,0:T(8,128)(2,1)} %copy.233) | copy-start | bytes 442372
  270.6 26.2 %copy-start.27 = (pred[128]{0:T(512)(128)(4,1)S(1)}, pred[128]{0:T(512)(128)(4,1)}, u32[]{:S(2)}) copy-start(pred[128]{0:T(512)(128)(4,1)} %get-tuple-element.258) | copy-start | bytes 388
  274.5 15.1 %collective-permute-start.2 = (bf16[4096,81]{0,1:T(8,128)(2,1)}, bf16[4096,81]{0,1:T(8,128)(2,1)S(1)}, u32[]{:S(2)}, u32[]{:S(2)}) collective-permute-start(bf16[4096,81]{0,1:T(8,128)(2,1)} %copy.234), channel_id=1, source_target_pairs={{0,1},{1,2},{2,3},{3,4},{4,5},{5,6},{6,7},{7,8},{8,9},{9,10},{10,1... | collective-permute-start | bytes 1990664 | tf_op jit(solution)/shard_map/ppermute | solution.py:36
  367.2 11.0 %copy-start.20 = (s32[128]{0:T(128)S(1)}, s32[128]{0:T(128)}, u32[]{:S(2)}) copy-start(s32[128]{0:T(128)} %copy-done.19) | copy-start | bytes 1540
  367.4 10.9 %copy-start.16 = (f32[2,256,64]{1,2,0:T(8,128)S(1)}, f32[2,256,64]{1,2,0:T(8,128)}, u32[]{:S(2)}) copy-start(f32[2,256,64]{1,2,0:T(8,128)} %custom-call.6) | copy-start | bytes 393220
  376.3 383.4 %collective-permute-start.3 = (bf16[4096,81]{0,1:T(8,128)(2,1)}, bf16[4096,81]{0,1:T(8,128)(2,1)}, u32[]{:S(2)}, u32[]{:S(2)}) collective-permute-start(bf16[4096,81]{0,1:T(8,128)(2,1)} %copy.244), channel_id=1, source_target_pairs={{1,0},{2,1},{3,2},{4,3},{5,4},{6,5},{7,6},{8,7},{9,8},{10,9},{11,1... | collective-permute-start | bytes 1990664 | tf_op jit(solution)/shard_map/ppermute | solution.py:36
  761.3 6.4 slice-start
  761.3 6.4 slice-start.1
  768.5 15.6 %copy-start.22 = (pred[128]{0:T(512)(128)(4,1)S(1)}, pred[128]{0:T(512)(128)(4,1)}, u32[]{:S(2)}) copy-start(pred[128]{0:T(512)(128)(4,1)} %copy-done.21) | copy-start | bytes 388
  768.5 15.6 %copy-start.24 = (pred[128]{0:T(512)(128)(4,1)S(1)}, pred[128]{0:T(512)(128)(4,1)}, u32[]{:S(2)}) copy-start(pred[128]{0:T(512)(128)(4,1)} %copy-done.23) | copy-start | bytes 388
  768.5 15.6 %copy-start.26 = (pred[128]{0:T(512)(128)(4,1)S(1)}, pred[128]{0:T(512)(128)(4,1)}, u32[]{:S(2)}) copy-start(pred[128]{0:T(512)(128)(4,1)} %copy-done.25) | copy-start | bytes 388
  (14 other events, 35.9 us)
Sparse Core Ops, SparseCore 0:
  452.5 305.5 all-reduce.5
where the time goes:
time: 937 us; the launch traced here: 929 us
  waiting for transfers between devices  308 us (33%)
  local copies, waits for them, and re-layouts  283 us (30%)
  other arithmetic  171 us (18%)
  blocking collectives  96.1 us (10%)
  matrix products  35.7 us (4%)
  between operations  15.9 us (2%)
  starting transfers between devices  15.6 us (2%)
    psum x1, waiting for transfers between devices, shards(): short_sum, medium_sum = lax.psum((short_grad, medium_grad), ('dp', 'ctx'))  302 us
    psum x1, blocking collectives, shards(): short_sum, medium_sum = lax.psum((short_grad, medium_grad), ('dp', 'ctx'))  76.4 us
    reshape x9, local copies, waits for them, and re-layouts, skewed(): tiled[..., :row_count * col_count]  64.2 us
    add x2, other arithmetic, short_pass(): summed = summed + jnp.where(tap_lag <= before, factor * window, 0.0)  45.1 us
    unnamed x98, local copies, waits for them, and re-layouts  28.6 us
    another operation x17, local copies, waits for them, and re-layouts, skewed(): tiled = jnp.tile(pattern, (1,) * len(lead_shape) + (row_count,))  26.9 us
    broadcast_in_dim x1, other arithmetic, shards(): grad_inputs.astype(jnp.bfloat16)[None]  25.3 us
    reduce_sum x2, other arithmetic, shards(): jnp.sum(jnp.where(tap_lag <= before, grad_filtered.astype(jnp.float32) *...  23.7 us
  transfers between devices with their start and end apart: 5, of which 2 were waited for; matrix products, arithmetic and copies ran while one was open for 26% of the time, Pallas kernels for 0%

commit v1 on v0

v1 whole, which is shorter than its diff:
```python
import functools
import math

import jax
import jax.numpy as jnp
from jax import lax
from jax.experimental import pallas as pl
from jax.experimental.pallas import tpu as pltpu
from jax.sharding import PartitionSpec as P

F32 = jnp.float32
BF16 = jnp.bfloat16
MESH = pl.DeviceIdType.MESH
LANES = 128
REACH = 22
TAIL_ROWS = 80
HEAD_ROWS = 16
LEAD = 8
HALF = 64


def iota(shape, dim):
    return lax.broadcasted_iota(jnp.int32, shape, dim)


def ones_where(condition, dtype=BF16):
    return jnp.where(condition, 1.0, 0.0).astype(dtype)


def dot(left, right):
    return jnp.dot(left, right, preferred_element_type=F32)


def dot_rows(left, right):
    return lax.dot_general(left, right, (((1,), (1,)), ((), ())), preferred_element_type=F32)


def column_of(row):
    return jnp.transpose(jnp.broadcast_to(row, (LANES, LANES)))


def tail_kernel(lengths_ref, raw_ref, tail_ref):
    live = lengths_ref[0, 0] + lengths_ref[0, 1]
    cap = raw_ref.shape[1]
    place = iota((TAIL_ROWS, cap), 0)
    column = iota((TAIL_ROWS, cap), 1)
    total = None
    for part in range(3):
        step = place - REACH * part
        pick = ones_where((step >= 0) & (step < REACH) & (column == live - REACH + step))
        term = dot(pick, raw_ref[part])
        total = term if total is None else total + term
    tail_ref[...] = total.astype(BF16)


def build_tail(lengths, raw, block=512):
    width = raw.shape[2]
    return pl.pallas_call(
        tail_kernel,
        grid=(width // block,),
        in_specs=[
            pl.BlockSpec(memory_space=pltpu.SMEM),
            pl.BlockSpec((3, raw.shape[1], block), lambda i: (0, 0, i)),
        ],
        out_specs=pl.BlockSpec((TAIL_ROWS, block), lambda i: (0, i)),
        out_shape=jax.ShapeDtypeStruct((TAIL_ROWS, width), BF16),
    )(lengths, raw)


def start_kernel(inner, lengths_ref, start_ref, mine, near, far, send, near_sem, far_sem):
    me = lax.axis_index("ctx")
    outer = lax.axis_size("ctx") // inner
    col, row = lax.rem(me, inner), lax.div(me, inner)
    barrier = pltpu.get_barrier_semaphore()
    for hop in range(1, inner):
        peer = row * inner + lax.rem(col + hop, inner)
        pl.semaphore_signal(barrier, inc=1, device_id={"ctx": peer}, device_id_type=MESH)
    for hop in range(1, outer):
        peer = lax.rem(row + hop, outer) * inner + col
        pl.semaphore_signal(barrier, inc=1, device_id={"ctx": peer}, device_id_type=MESH)
    pl.semaphore_wait(barrier, inner + outer - 2)
    lengths = lengths_ref[...]
    live = jnp.broadcast_to(lengths[0:1, 0:1] + lengths[0:1, 1:2], (8, LANES))
    mine[0] = live
    copies = []
    for hop in range(1, inner):
        peer = row * inner + lax.rem(col + hop, inner)
        copy = pltpu.make_async_remote_copy(
            mine.at[0],
            near.at[inner - hop],
            send.at[hop],
            near_sem.at[inner - hop],
            device_id={"ctx": peer},
            device_id_type=MESH,
        )
        copy.start()
        copies.append(copy)
    for copy in copies:
        copy.wait()
    before = jnp.zeros((8, LANES), jnp.int32)
    whole = live
    for hop in range(1, inner):
        value = near[hop]
        whole = whole + value
        before = before + value * jnp.where(col + hop >= inner, 1, 0)
    mine[1] = whole
    copies = []
    for hop in range(1, outer):
        peer = lax.rem(row + hop, outer) * inner + col
        copy = pltpu.make_async_remote_copy(
            mine.at[1],
            far.at[outer - hop],
            send.at[inner + hop],
            far_sem.at[outer - hop],
            device_id={"ctx": peer},
            device_id_type=MESH,
        )
        copy.start()
        copies.append(copy)
    for copy in copies:
        copy.wait()
    for hop in range(1, outer):
        before = before + far[hop] * jnp.where(row + hop >= outer, 1, 0)
    start_ref[...] = before


def block_start(lengths, inner=8):
    outer = lax.axis_size("ctx") // inner
    return pl.pallas_call(
        functools.partial(start_kernel, inner),
        in_specs=[pl.BlockSpec(memory_space=pltpu.VMEM)],
        out_specs=pl.BlockSpec(memory_space=pltpu.VMEM),
        out_shape=jax.ShapeDtypeStruct((8, LANES), jnp.int32),
        scratch_shapes=[
            pltpu.VMEM((2, 8, LANES), jnp.int32),
            pltpu.VMEM((inner, 8, LANES), jnp.int32),
            pltpu.VMEM((outer, 8, LANES), jnp.int32),
            pltpu.SemaphoreType.DMA((inner + outer,)),
            pltpu.SemaphoreType.DMA((inner,)),
            pltpu.SemaphoreType.DMA((outer,)),
        ],
        compiler_params=pltpu.CompilerParams(collective_id=0, has_side_effects=True),
    )(lengths)


def widened_taps(short_ref, block, lanes):
    groups = short_ref.shape[2]
    spread = ones_where(iota((groups, lanes), 0) == (block * lanes + iota((groups, lanes), 1)) // 16)
    return [dot(short_ref[part].astype(BF16), spread) for part in range(3)]


def forward_kernel(
    drift_ref,
    lengths_ref,
    raw_ref,
    tail_ref,
    head_ref,
    short_ref,
    span_ref,
    cot_ref,
    packed_ref,
    cot_out_ref,
    filtered_ref,
    mixed_ref,
    weighted_ref,
    own_pick,
    edge_pick,
    masks,
    rows,
):
    cap = raw_ref.shape[1]
    count = cot_ref.shape[1]
    block = pl.program_id(0)

    @pl.when(block == 0)
    def _():
        drift = drift_ref[0, 0]
        live = lengths_ref[0, 0] + lengths_ref[0, 1]
        token = iota((LEAD + count, cap), 0) - LEAD
        column = iota((LEAD + count, cap), 1)
        own_pick[...] = ones_where((column == token - drift) & (column < live))
        token = iota((LEAD + count, LANES), 0) - LEAD
        column = iota((LEAD + count, LANES), 1)
        for part in range(3):
            late = token - drift + REACH
            from_tail = (late >= 0) & (late < REACH) & (column == REACH * part + late)
            over = token - drift - live
            from_head = (over >= 0) & (column == TAIL_ROWS + HEAD_ROWS * part + over)
            edge_pick[part] = ones_where(from_tail | from_head)
        before = column_of(span_ref[0:1])
        for lag in range(1, 7):
            masks[lag - 1] = ones_where(before >= lag, F32)

    taps = widened_taps(short_ref, block, LANES)
    edges = jnp.concatenate([tail_ref[...]] + [head_ref[part] for part in range(3)], axis=0)
    filtered = []
    for part in range(3):
        packed = dot(own_pick[...], raw_ref[part]) + dot(edge_pick[part], edges)
        rows[part] = packed
        packed_ref[part] = packed[LEAD:].astype(BF16)
        total = taps[part][0:1] * packed[LEAD:]
        for lag in range(1, 7):
            window = rows[part, LEAD - lag : LEAD - lag + count]
            total = total + taps[part][lag : lag + 1] * (masks[lag - 1] * window)
        filtered.append(total)
    filtered_ref[0] = filtered[1]
    filtered_ref[1] = filtered[2]
    mixed_ref[...] = (filtered[1] * filtered[2]).astype(BF16)
    cot = jnp.transpose(cot_ref[...].astype(F32))
    cot_out_ref[...] = cot.astype(BF16)
    weighted_ref[...] = (cot * filtered[0]).astype(BF16)


def forward(drift, lengths, raw, tail, head, short, span, cot):
    cap, width = raw.shape[1:]
    count = cot.shape[1]
    smem = pl.BlockSpec(memory_space=pltpu.SMEM)
    by_lane = lambda *lead: pl.BlockSpec(lead + (LANES,), lambda i: (0,) * len(lead) + (i,))
    whole = lambda a: pl.BlockSpec(a.shape, lambda i: (0,) * a.ndim)
    return pl.pallas_call(
        forward_kernel,
        grid=(width // LANES,),
        in_specs=[
            smem,
            smem,
            by_lane(3, cap),
            by_lane(TAIL_ROWS),
            by_lane(3, HEAD_ROWS),
            whole(short),
            whole(span),
            pl.BlockSpec((LANES, count), lambda i: (i, 0)),
        ],
        out_specs=[
            by_lane(3, count),
            by_lane(count),
            by_lane(2, count),
            by_lane(count),
            by_lane(count),
        ],
        out_shape=[
            jax.ShapeDtypeStruct((3, count, width), BF16),
            jax.ShapeDtypeStruct((count, width), BF16),
            jax.ShapeDtypeStruct((2, count, width), F32),
            jax.ShapeDtypeStruct((count, width), BF16),
            jax.ShapeDtypeStruct((count, width), BF16),
        ],
        scratch_shapes=[
            pltpu.VMEM((LEAD + count, cap), BF16),
            pltpu.VMEM((3, LEAD + count, LANES), BF16),
            pltpu.VMEM((6, count, LANES), F32),
            pltpu.VMEM((3, LEAD + count, LANES), F32),
        ],
    )(drift, lengths, raw, tail, head, short, span, cot)


def medium_kernel(
    medium_ref,
    span_ref,
    cot_ref,
    filtered_ref,
    mixed_ref,
    mixed_halo_ref,
    weighted_ref,
    weighted_halo_ref,
    grad_ref,
    corr_ref,
    fore_rows,
    back_rows,
    fore_mask,
    back_mask,
    back_mask32,
):
    block = pl.program_id(0)
    taps = medium_ref.shape[0]

    @pl.when(block == 0)
    def _():
        source = iota((taps, LANES), 0)
        lane = iota((taps, LANES), 1)
        filt = medium_ref[...].astype(BF16)
        across = lambda pick: lax.dot_general(
            filt, pick, (((0,), (0,)), ((), ())), preferred_element_type=F32
        )
        fore_rows[...] = across(ones_where(lane == taps - source))
        back_rows[...] = across(ones_where(lane == source))
        before, after = column_of(span_ref[0:1]), column_of(span_ref[1:2])
        row = iota((HALF, LANES), 0)
        lane = iota((HALF, LANES), 1)
        for half in range(2):
            part = slice(HALF * half, HALF * half + HALF)
            lag = row + HALF - lane
            fore_mask[half] = ones_where((lag >= 0) & (lag < taps) & (lag <= before[part]))
            lag = lane - row
            back = (lag >= 0) & (lag < taps) & (lag <= after[part])
            back_mask[half] = ones_where(back)
            back_mask32[half] = ones_where(back, F32)

    fore = fore_rows[pl.ds(pl.multiple_of(block * 8, 8), 8)]
    back = back_rows[pl.ds(pl.multiple_of(block * 8, 8), 8)]
    toeplitz = lambda rows, g: pltpu.roll(
        jnp.broadcast_to(rows[g : g + 1], (HALF, LANES)).astype(BF16), 0, 1, stride=1, stride_axis=0
    )
    fores = [toeplitz(fore, g) for g in range(8)]
    backs = [toeplitz(back, g) for g in range(8)]
    group_of = iota((HALF, LANES), 1) // 16
    mixed = mixed_ref[...]
    weighted = weighted_ref[...]
    mixed_ext = jnp.concatenate([mixed_halo_ref[...], mixed], axis=0)
    weighted_ext = jnp.concatenate([weighted, weighted_halo_ref[...]], axis=0)
    corr = [None] * 8
    for half in range(2):
        part = slice(HALF * half, HALF * half + HALF)
        window = slice(HALF * half, HALF * half + 2 * HALF)
        mask = fore_mask[half]
        bands = jnp.concatenate([f * mask for f in fores], axis=0)
        every = dot(bands, mixed_ext[window])
        response = every[:HALF]
        for g in range(1, 8):
            response = jnp.where(group_of == g, every[HALF * g : HALF * g + HALF], response)
        mask = back_mask[half]
        bands = jnp.concatenate([b * mask for b in backs], axis=0)
        every = dot(bands, weighted_ext[window])
        spread = every[:HALF]
        for g in range(1, 8):
            spread = jnp.where(group_of == g, every[HALF * g : HALF * g + HALF], spread)
        grad_ref[0, part] = (cot_ref[part].astype(F32) * response).astype(BF16)
        grad_ref[1, part] = (spread * filtered_ref[1, part]).astype(BF16)
        grad_ref[2, part] = (spread * filtered_ref[0, part]).astype(BF16)
        zero = jnp.zeros((HALF, LANES), BF16)
        alone = jnp.concatenate(
            [jnp.where(group_of == g, mixed[part], zero) for g in range(8)], axis=0
        )
        every = dot_rows(alone, weighted_ext[window])
        for g in range(8):
            term = every[HALF * g : HALF * g + HALF] * back_mask32[half]
            corr[g] = term if half == 0 else corr[g] + term
    for g in range(8):
        total = corr[g][0:8]
        for strip in range(1, 8):
            total = total + pltpu.roll(corr[g][8 * strip : 8 * strip + 8], LANES - 8 * strip, 1)
        corr_ref[g] = total


def medium(filt, span, cot, filtered, mixed, mixed_halo, weighted, weighted_halo):
    taps, groups = filt.shape
    count, width = mixed.shape
    by_lane = lambda *lead: pl.BlockSpec(lead + (LANES,), lambda i: (0,) * len(lead) + (i,))
    whole = lambda a: pl.BlockSpec(a.shape, lambda i: (0,) * a.ndim)
    return pl.pallas_call(
        medium_kernel,
        grid=(width // LANES,),
        in_specs=[
            whole(filt),
            whole(span),
            by_lane(count),
            by_lane(2, count),
            by_lane(count),
            by_lane(HALF),
            by_lane(count),
            by_lane(HALF),
        ],
        out_specs=[
            by_lane(3, count),
            pl.BlockSpec((8, 8, LANES), lambda i: (i, 0, 0)),
        ],
        out_shape=[
            jax.ShapeDtypeStruct((3, count, width), BF16),
            jax.ShapeDtypeStruct((groups, 8, LANES), F32),
        ],
        scratch_shapes=[
            pltpu.VMEM((groups, LANES), F32),
            pltpu.VMEM((groups, LANES), F32),
            pltpu.VMEM((2, HALF, LANES), BF16),
            pltpu.VMEM((2, HALF, LANES), BF16),
            pltpu.VMEM((2, HALF, LANES), F32),
        ],
    )(filt, span, cot, filtered, mixed, mixed_halo, weighted, weighted_halo)


def backward_kernel(
    short_ref, span_ref, packed_ref, grad_ref, grad_halo_ref, corr_ref, out_ref, sums_ref, masks, rows
):
    block = pl.program_id(0)
    count = packed_ref.shape[1]
    groups = short_ref.shape[2]

    @pl.when(block == 0)
    def _():
        after = column_of(span_ref[1:2])
        for lag in range(1, 7):
            masks[lag - 1] = ones_where(after >= lag, F32)
        sums_ref[0:24] = jnp.zeros((24, groups), F32)
        taps = 64
        total = None
        for row in range(8):
            strip = corr_ref[:, row, :]
            strip = strip if row == 0 else pltpu.roll(strip, LANES - row, 1)
            total = strip if total is None else total + strip
        sums_ref[24 : 24 + taps] = jnp.transpose(total)[:taps]

    taps = widened_taps(short_ref, block, LANES)
    sums = []
    for part in range(3):
        rows[part, 0:count] = grad_ref[part].astype(F32)
        rows[part, count : count + 16] = grad_halo_ref[part].astype(F32)
        packed = packed_ref[part].astype(F32)
        total = None
        for lag in range(7):
            window = rows[part, lag : lag + count]
            if lag:
                window = masks[lag - 1] * window
            term = taps[part][lag : lag + 1] * window
            total = term if total is None else total + term
            sums.append(jnp.sum(packed * window, axis=0, keepdims=True))
        out_ref[part] = jnp.transpose(total).astype(BF16)
    sums = jnp.concatenate(sums + [jnp.zeros((3, LANES), F32)], axis=0)
    high = sums.astype(BF16)
    low = (sums - high.astype(F32)).astype(BF16)
    gather = ones_where(
        iota((LANES, groups), 1) == (block * LANES + iota((LANES, groups), 0)) // 16
    )
    sums_ref[0:24] = sums_ref[0:24] + dot(high, gather) + dot(low, gather)


def backward(short, span, packed, grad, grad_halo, corr):
    count, width = packed.shape[1:]
    groups = short.shape[2]
    by_lane = lambda *lead: pl.BlockSpec(lead + (LANES,), lambda i: (0,) * len(lead) + (i,))
    whole = lambda a: pl.BlockSpec(a.shape, lambda i: (0,) * a.ndim)
    return pl.pallas_call(
        backward_kernel,
        grid=(width // LANES,),
        in_specs=[
            whole(short),
            whole(span),
            by_lane(3, count),
            by_lane(3, count),
            by_lane(3, 16),
            whole(corr),
        ],
        out_specs=[
            pl.BlockSpec((3, LANES, count), lambda i: (0, i, 0)),
            pl.BlockSpec((88, groups), lambda i: (0, 0)),
        ],
        out_shape=[
            jax.ShapeDtypeStruct((3, width, count), BF16),
            jax.ShapeDtypeStruct((88, groups), F32),
        ],
        scratch_shapes=[
            pltpu.VMEM((6, count, LANES), F32),
            pltpu.VMEM((3, count + 16, LANES), F32),
        ],
    )(short, span, packed, grad, grad_halo, corr)


def total_kernel(scale, part_ref, short_out, medium_out, mine, first, second, result, send, sem1, sem2, sem3):
    x, ctx = lax.axis_index("dp"), lax.axis_index("ctx")
    z, yc = lax.div(ctx, 8), lax.rem(ctx, 8)
    y, core = lax.div(yc, 2), lax.rem(yc, 2)
    place1 = z * 2 + core
    place2 = x * 4 + y

    def peer1(other):
        return {"dp": x, "ctx": lax.div(other, 2) * 8 + y * 2 + lax.rem(other, 2)}

    def peer2(other):
        return {"dp": lax.div(other, 4), "ctx": z * 8 + lax.rem(other, 4) * 2 + core}

    barrier = pltpu.get_barrier_semaphore()
    for hop in range(1, 16):
        pl.semaphore_signal(
            barrier, inc=1, device_id=peer1(lax.rem(place1 + hop, 16)), device_id_type=MESH
        )
        pl.semaphore_signal(
            barrier, inc=1, device_id=peer2(lax.rem(place2 + hop, 16)), device_id_type=MESH
        )
    groups = part_ref.shape[1]
    for piece in range(11):
        mine[piece] = part_ref[8 * piece : 8 * piece + 8]
    for piece in range(11, 16):
        mine[piece] = jnp.zeros((8, groups), F32)
    pl.semaphore_wait(barrier, 30)

    def exchange(source, target, sems, peer, place):
        copies = []
        for hop in range(1, 16):
            other = lax.rem(place + hop, 16)
            copy = pltpu.make_async_remote_copy(
                source(other),
                target(hop),
                send.at[hop],
                sems.at[16 - hop],
                device_id=peer(other),
                device_id_type=MESH,
            )
            copy.start()
            copies.append(copy)
        for copy in copies:
            copy.wait()

    exchange(lambda other: mine.at[other], lambda hop: first.at[16 - hop], sem1, peer1, place1)
    total = mine[place1]
    for hop in range(1, 16):
        total = total + first[hop]
    second[0] = total
    exchange(lambda other: second.at[0], lambda hop: second.at[16 - hop], sem2, peer2, place2)
    total = jnp.zeros((8, groups), F32)
    for other in range(16):
        total = total + second[lax.rem(other - place2 + 16, 16)]
    result[place1] = total * (1.0 / scale)
    exchange(lambda other: result.at[place1], lambda hop: result.at[place1], sem3, peer1, place1)
    short_out[...] = jnp.concatenate([result[piece] for piece in range(3)], axis=0)
    for piece in range(3, 11):
        medium_out[8 * (piece - 3) : 8 * (piece - 3) + 8] = result[piece]


def total_over_devices(part, scale):
    groups = part.shape[1]
    vmem = pl.BlockSpec(memory_space=pltpu.VMEM)
    dma = pltpu.SemaphoreType.DMA((16,))
    return pl.pallas_call(
        functools.partial(total_kernel, scale),
        in_specs=[vmem],
        out_specs=[vmem, vmem],
        out_shape=[
            jax.ShapeDtypeStruct((24, groups), F32),
            jax.ShapeDtypeStruct((64, groups), F32),
        ],
        scratch_shapes=[
            pltpu.VMEM((16, 8, groups), F32),
            pltpu.VMEM((16, 8, groups), F32),
            pltpu.VMEM((16, 8, groups), F32),
            pltpu.VMEM((16, 8, groups), F32),
            dma,
            dma,
            dma,
            dma,
        ],
        compiler_params=pltpu.CompilerParams(collective_id=1, has_side_effects=True),
    )(part)


def passed_along(block, distance):
    devices = range(lax.axis_size("ctx"))
    route = [(i - distance, i) for i in devices if i - distance in devices]
    return lax.ppermute(block, "ctx", route)


def shards(raw_qkv, block_lengths, short_filter, medium_filter, doc_span, cotangent):
    count = cotangent.shape[2]
    groups = medium_filter.shape[0]
    group_size = cotangent.shape[1] // groups
    raw = jnp.transpose(raw_qkv[0], (0, 2, 1))
    lengths = block_lengths[0]
    short = jnp.pad(jnp.transpose(short_filter, (0, 2, 1)), ((0, 0), (0, 1), (0, 0)))
    filt = jnp.transpose(medium_filter)
    span = doc_span[0]
    cot = cotangent[0]

    tail = passed_along(build_tail(lengths, raw), 1)
    head = passed_along(raw[:, :HEAD_ROWS], -1)
    start = block_start(lengths)[0:1, 0:1]
    drift = start - lax.axis_index("ctx") * count
    packed, cot_rows, filtered, mixed, weighted = forward(
        drift, lengths, raw, tail, head, short, span, cot
    )
    mixed_halo = passed_along(mixed[count - HALF :], 1)
    weighted_halo = passed_along(weighted[:HALF], -1)
    grad, corr = medium(filt, span, cot_rows, filtered, mixed, mixed_halo, weighted, weighted_halo)
    grad_halo = passed_along(grad[:, :16], -1)
    out, sums = backward(short, span, packed, grad, grad_halo, corr)
    scale = math.sqrt(lax.axis_size("dp") * lax.axis_size("ctx") * count * group_size)
    short_sum, medium_sum = total_over_devices(sums, scale)
    short_grad = jnp.transpose(short_sum[:21].reshape(3, 7, groups), (0, 2, 1))
    return (out[None], short_grad, jnp.transpose(medium_sum))


def solution(mesh):
    return jax.shard_map(
        shards,
        mesh=mesh,
        in_specs=(
            P("dp", None, None, "ctx"),
            P("dp", "ctx", None),
            P(),
            P(),
            P("dp", None, "ctx"),
            P("dp", None, "ctx"),
        ),
        out_specs=(P("dp", None, None, "ctx"), P(), P()),
        check_vma=False,
    )
```

time: 937 us -> 171 us (0.18)
  waiting for transfers between devices: 308 us -> 14 us
  local copies, waits for them, and re-layouts: 283 us -> 11.4 us
  other arithmetic: 171 us -> 0 us
  Pallas kernels: 0 us -> 128 us
  blocking collectives: 96.1 us -> 0 us
  matrix products: 35.7 us -> 0 us
  between operations: 15.9 us -> 1.39 us
    psum x1 -> x0, waiting for transfers between devices: 302 us -> none  [shards(): short_sum, medium_sum = lax.psum((short_grad, medium_grad), ('dp', 'ctx'))]
    pallas_call x0 -> x6, Pallas kernels: none -> 128 us  [the longest x1 28.3 us: total_over_devices(): pl.pallas_call(functools.partial(total_kernel, scale), in_specs=[vmem], o...]
    reshape x27 -> x1, local copies, waits for them, and re-layouts: 106 us -> 1.35 us  [shards(): short_grad = jnp.transpose(short_sum[:21].reshape(3, 7, groups), (0, 2, 1))]
    psum x1 -> x0, blocking collectives: 76.4 us -> none  [shards(): short_sum, medium_sum = lax.psum((short_grad, medium_grad), ('dp', 'ctx'))]
    add x3 -> x0, other arithmetic: 45.1 us -> none  [the longest x2 45.1 us: short_pass(): summed = summed + jnp.where(tap_lag <= before, factor * window, 0.0)]
    dot_general x5 -> x0, matrix products: 35.7 us -> none  [the longest x2 12.5 us: block_out(): jnp.einsum('gct,gcu->gtu', left_op, right_op, preferred_element_type=jnp....]
    another operation x21 -> x0, local copies, waits for them, and re-layouts: 32.9 us -> none  [the longest x17 26.9 us: skewed(): tiled = jnp.tile(pattern, (1,) * len(lead_shape) + (row_count,))]
    reduce_sum x13 -> x0, other arithmetic: 32 us -> none  [the longest x2 23.7 us: shards(): jnp.sum(jnp.where(tap_lag <= before, grad_filtered.astype(jnp.float32) *...]
  transfers between devices with their start and end apart: 5 -> 5, of which waited for: 2 -> 3; matrix products, arithmetic and copies ran while one was open for 26% -> 2% of each run, Pallas kernels for 0% -> 11%
where the time goes in v1:
time: 171 us; the launch traced here: 168 us
  Pallas kernels  128 us (75%)
  starting transfers between devices  14 us (8%)
  waiting for transfers between devices  14 us (8%)
  local copies, waits for them, and re-layouts  11.4 us (7%)
    pallas_call x1, Pallas kernels, total_over_devices(): pl.pallas_call(functools.partial(total_kernel, scale), in_specs=[vmem], o...  28.3 us
    pallas_call x1, Pallas kernels, backward(): pl.pallas_call(backward_kernel, grid=(width // LANES,), in_specs=[whole(s...  25.5 us
    pallas_call x1, Pallas kernels, medium(): pl.pallas_call(medium_kernel, grid=(width // LANES,), in_specs=[whole(fil...  24.7 us
    pallas_call x1, Pallas kernels, forward(): pl.pallas_call(forward_kernel, grid=(width // LANES,), in_specs=[smem, sm...  24.1 us
    pallas_call x1, Pallas kernels, block_start(): pl.pallas_call(functools.partial(start_kernel, inner), in_specs=[pl.Block...  18.6 us
    ppermute x5, waiting for transfers between devices, passed_along(): return lax.ppermute(block, 'ctx', route)  14 us
    ppermute x5, starting transfers between devices, passed_along(): return lax.ppermute(block, 'ctx', route)  14 us
    pallas_call x1, Pallas kernels, build_tail(): pl.pallas_call(tail_kernel, grid=(width // block,), in_specs=[pl.BlockSpe...  6.49 us
  transfers between devices with their start and end apart: 5, of which 3 were waited for; matrix products, arithmetic and copies ran while one was open for 2% of the time, Pallas kernels for 11%

profile of v1, /device:TPU:1, one launch (start us, length us, event | category | flops | bytes accessed | tf_op | source)
XLA Modules:
  0.0 168.4 jit_solution(14997431431246737470)
XLA Ops:
  0.6 0.0 copy-start.5
  0.6 6.5 %shard_map.86 = bf16[80,4096]{1,0:T(8,128)(2,1)} custom-call(s32[1,2]{1,0:T(1,128)} %bitcast.25, bf16[3,160,4096]{2,1,0:T(8,128)(2,1)} %bitcast.13), custom_call_target="tpu_custom_call" | custom-call | tf_op jit(solution)/shard_map/pallas_call | solution.py:58
  7.1 4.6 %collective-permute-start = (bf16[80,4096]{1,0:T(8,128)(2,1)}, bf16[80,4096]{1,0:T(8,128)(2,1)S(1)}, u32[]{:S(2)}, u32[]{:S(2)}) collective-permute-start(bf16[80,4096]{1,0:T(8,128)(2,1)} %shard_map.86), channel_id=1, source_target_pairs={{0,1},{1,2},{2,3},{3,4},{4,5},{5,6},{6,7},{7,8},{8,9},{9,10},{10,1... | collective-permute-start | bytes 1966088 | tf_op jit(solution)/shard_map/ppermute | solution.py:546
  11.7 1.0 slice.24
  12.7 1.9 %collective-permute-start.1 = (bf16[3,16,4096]{2,1,0:T(8,128)(2,1)S(1)}, bf16[3,16,4096]{2,1,0:T(8,128)(2,1)S(1)}, u32[]{:S(2)}, u32[]{:S(2)}) collective-permute-start(bf16[3,16,4096]{2,1,0:T(8,128)(2,1)S(1)} %slice.24), channel_id=1, source_target_pairs={{1,0},{2,1},{3,2},{4,3},{5,4},{6,5},{7,6},{8,7},{9,8},{10,9},{11,1... | collective-permute-start | bytes 1179656 | tf_op jit(solution)/shard_map/ppermute | solution.py:546
  14.7 18.6 %shard_map.85 = s32[8,128]{1,0:T(8,128)} custom-call(s32[1,2]{1,0:T(1,128)} %bitcast.26), custom_call_target="tpu_custom_call" | custom-call | tf_op jit(solution)/shard_map/pallas_call | solution.py:129
  33.2 1.2 slice.18
  35.1 0.0 copy-done.5
  35.1 0.6 pad.4.short_ref
  35.7 0.0 collective-permute-done.1.head_ref
  35.7 0.0 collective-permute-done.tail_ref
  35.7 0.0 copy-start
  35.7 0.8 copy-done.4
  36.5 0.2 copy-done
  36.7 24.1 %shard_map.87 = (bf16[3,128,4096]{2,1,0:T(8,128)(2,1)}, bf16[128,4096]{1,0:T(8,128)(2,1)}, f32[2,128,4096]{2,1,0:T(8,128)}, bf16[128,4096]{1,0:T(8,128)(2,1)}, bf16[128,4096]{1,0:T(8,128)(2,1)}) custom-call(s32[1,1]{1,0:T(1,128)S(6)} %sub.7.drift_ref, s32[1,2]{1,0:T(1,128)} %bitcast.27, bf16[3,160,4096]{2,1,0:T(8,128)(2,1)} %bitcast.15, ...), custom_call_target="tpu_custom_call" | custom-call | tf_op jit(solution)/shard_map/pallas_call | solution.py:220
  60.8 1.1 slice.20
  61.9 1.1 slice.21
  63.0 3.2 %collective-permute-start.3 = (bf16[64,4096]{1,0:T(8,128)(2,1)S(1)}, bf16[64,4096]{1,0:T(8,128)(2,1)S(1)}, u32[]{:S(2)}, u32[]{:S(2)}) collective-permute-start(bf16[64,4096]{1,0:T(8,128)(2,1)S(1)} %slice.21), channel_id=1, source_target_pairs={{1,0},{2,1},{3,2},{4,3},{5,4},{6,5},{7,6},{8,7},{9,8},{10,9},{11,1... | collective-permute-start | bytes 1572872 | tf_op jit(solution)/shard_map/ppermute | solution.py:546
  66.2 2.4 %collective-permute-start.2 = (bf16[64,4096]{1,0:T(8,128)(2,1)S(1)}, bf16[64,4096]{1,0:T(8,128)(2,1)S(1)}, u32[]{:S(2)}, u32[]{:S(2)}) collective-permute-start(bf16[64,4096]{1,0:T(8,128)(2,1)S(1)} %slice.20), channel_id=1, source_target_pairs={{0,1},{1,2},{2,3},{3,4},{4,5},{5,6},{6,7},{7,8},{8,9},{9,10},{10,1... | collective-permute-start | bytes 1572872 | tf_op jit(solution)/shard_map/ppermute | solution.py:546
  68.6 4.9 %collective-permute-done.3.weighted_halo_ref = bf16[64,4096]{1,0:T(8,128)(2,1)S(1)} collective-permute-done((bf16[64,4096]{1,0:T(8,128)(2,1)S(1)}, bf16[64,4096]{1,0:T(8,128)(2,1)S(1)}, u32[]{:S(2)}, u32[]{:S(2)}) %collective-permute-start.3) | collective-permute-done | bytes 524320 | tf_op jit(solution)/shard_map/ppermute | solution.py:546
  73.5 1.2 collective-permute-done.2.mixed_halo_ref
  74.7 0.0 copy-done.1
  74.7 0.8 copy-done.2
  75.5 24.7 %shard_map.88 = (bf16[3,128,4096]{2,1,0:T(8,128)(2,1)}, f32[256,8,128]{2,1,0:T(8,128)}) custom-call(f32[64,256]{1,0:T(8,128)} %bitcast.17, s32[2,128]{1,0:T(2,128)} %bitcast.23, bf16[128,4096]{1,0:T(8,128)(2,1)} %get-tuple-element.15.cot_ref, f32[2,128,4096]{2,1,0:T(8,128)} %get-tuple-element.16.filtered_ref, bf16[128,4096]{1,0:T(8,128)(2,1)} %get-tuple-element.17.mixed_ref, ...), custom_call_target="tpu_custom_call" | custom-call | tf_op jit(solution)/shard_map/pallas_call | solution.py:349
  100.2 1.0 slice.22
  101.2 1.9 %collective-permute-start.4 = (bf16[3,16,4096]{2,1,0:T(8,128)(2,1)S(1)}, bf16[3,16,4096]{2,1,0:T(8,128)(2,1)S(1)}, u32[]{:S(2)}, u32[]{:S(2)}) collective-permute-start(bf16[3,16,4096]{2,1,0:T(8,128)(2,1)S(1)} %slice.22), channel_id=1, source_target_pairs={{1,0},{2,1},{3,2},{4,3},{5,4},{6,5},{7,6},{8,7},{9,8},{10,9},{11,1... | collective-permute-start | bytes 1179656 | tf_op jit(solution)/shard_map/ppermute | solution.py:546
  103.1 7.9 %collective-permute-done.4.grad_halo_ref = bf16[3,16,4096]{2,1,0:T(8,128)(2,1)S(1)} collective-permute-done((bf16[3,16,4096]{2,1,0:T(8,128)(2,1)S(1)}, bf16[3,16,4096]{2,1,0:T(8,128)(2,1)S(1)}, u32[]{:S(2)}, u32[]{:S(2)}) %collective-permute-start.4) | collective-permute-done | bytes 393248 | tf_op jit(solution)/shard_map/ppermute | solution.py:546
  111.0 0.8 copy-done.3
  111.8 25.5 %shard_map.89 = (bf16[3,4096,128]{2,1,0:T(8,128)(2,1)}, f32[88,256]{1,0:T(8,128)}) custom-call(f32[3,8,256]{2,1,0:T(8,128)} %pad.4.short_ref, s32[2,128]{1,0:T(2,128)} %bitcast.24, bf16[3,128,4096]{2,1,0:T(8,128)(2,1)} %get-tuple-element.14.packed_ref, bf16[3,128,4096]{2,1,0:T(8,128)(2,1)} %get-tuple-element.19.grad_ref, bf16[3,16,4096]{2,1,0:T(8,128)(2,1)} %copy-done.3, ...), custom_call_target="tpu_custom_call" | custom-call | tf_op jit(solution)/shard_map/pallas_call | solution.py:430
  137.3 28.3 %shard_map.90 = (f32[24,256]{1,0:T(8,128)}, f32[64,256]{1,0:T(8,128)}) custom-call(f32[88,256]{1,0:T(8,128)} %get-tuple-element.22.part_ref), custom_call_target="tpu_custom_call" | custom-call | tf_op jit(solution)/shard_map/pallas_call | solution.py:521
  165.6 1.3 reshape.9
  167.0 1.5 copy.10
  (4 shorter events, 0.0 us)
Async XLA Ops:
  0.6 34.5 %copy-start.5 = (f32[3,256,7]{1,2,0:T(8,128)S(1)}, f32[3,256,7]{1,2,0:T(8,128)}, u32[]{:S(2)}) copy-start(f32[3,256,7]{1,2,0:T(8,128)} %param.8) | copy-start | bytes 64516
  7.1 28.6 %collective-permute-start = (bf16[80,4096]{1,0:T(8,128)(2,1)}, bf16[80,4096]{1,0:T(8,128)(2,1)S(1)}, u32[]{:S(2)}, u32[]{:S(2)}) collective-permute-start(bf16[80,4096]{1,0:T(8,128)(2,1)} %shard_map.86), channel_id=1, source_target_pairs={{0,1},{1,2},{2,3},{3,4},{4,5},{5,6},{6,7},{7,8},{8,9},{9,10},{10,1... | collective-permute-start | bytes 1966088 | tf_op jit(solution)/shard_map/ppermute | solution.py:546
  12.7 23.0 %collective-permute-start.1 = (bf16[3,16,4096]{2,1,0:T(8,128)(2,1)S(1)}, bf16[3,16,4096]{2,1,0:T(8,128)(2,1)S(1)}, u32[]{:S(2)}, u32[]{:S(2)}) collective-permute-start(bf16[3,16,4096]{2,1,0:T(8,128)(2,1)S(1)} %slice.24), channel_id=1, source_target_pairs={{1,0},{2,1},{3,2},{4,3},{5,4},{6,5},{7,6},{8,7},{9,8},{10,9},{11,1... | collective-permute-start | bytes 1179656 | tf_op jit(solution)/shard_map/ppermute | solution.py:546
  35.7 0.8 copy-start.4
  35.7 1.0 copy-start
  63.0 10.5 %collective-permute-start.3 = (bf16[64,4096]{1,0:T(8,128)(2,1)S(1)}, bf16[64,4096]{1,0:T(8,128)(2,1)S(1)}, u32[]{:S(2)}, u32[]{:S(2)}) collective-permute-start(bf16[64,4096]{1,0:T(8,128)(2,1)S(1)} %slice.21), channel_id=1, source_target_pairs={{1,0},{2,1},{3,2},{4,3},{5,4},{6,5},{7,6},{8,7},{9,8},{10,9},{11,1... | collective-permute-start | bytes 1572872 | tf_op jit(solution)/shard_map/ppermute | solution.py:546
  66.2 8.5 %collective-permute-start.2 = (bf16[64,4096]{1,0:T(8,128)(2,1)S(1)}, bf16[64,4096]{1,0:T(8,128)(2,1)S(1)}, u32[]{:S(2)}, u32[]{:S(2)}) collective-permute-start(bf16[64,4096]{1,0:T(8,128)(2,1)S(1)} %slice.20), channel_id=1, source_target_pairs={{0,1},{1,2},{2,3},{3,4},{4,5},{5,6},{6,7},{7,8},{8,9},{9,10},{10,1... | collective-permute-start | bytes 1572872 | tf_op jit(solution)/shard_map/ppermute | solution.py:546
  73.5 1.2 copy-start.1
  74.7 0.8 copy-start.2
  101.2 9.8 %collective-permute-start.4 = (bf16[3,16,4096]{2,1,0:T(8,128)(2,1)S(1)}, bf16[3,16,4096]{2,1,0:T(8,128)(2,1)S(1)}, u32[]{:S(2)}, u32[]{:S(2)}) collective-permute-start(bf16[3,16,4096]{2,1,0:T(8,128)(2,1)S(1)} %slice.22), channel_id=1, source_target_pairs={{1,0},{2,1},{3,2},{4,3},{5,4},{6,5},{7,6},{8,7},{9,8},{10,9},{11,1... | collective-permute-start | bytes 1179656 | tf_op jit(solution)/shard_map/ppermute | solution.py:546
  111.0 0.8 copy-start.3

commit v2 on v0

v2 whole, which is shorter than its diff:
```python
import functools
import math
import types

import jax
import jax.numpy as jnp
from jax import lax
from jax.experimental import pallas as pl
from jax.experimental.pallas import tpu as pltpu
from jax.sharding import PartitionSpec as P

F32 = jnp.float32
BF16 = jnp.bfloat16
I32 = jnp.int32
MESH = pl.DeviceIdType.MESH
LANES = 128
WIDE = 256
REACH = 22
TAIL_ROWS = 80
HEAD_ROWS = 16
LEAD = 8
HALF = 64
COUNT = 128
TEAM = 16
INNER = 8


def iota(shape, dim):
    return lax.broadcasted_iota(I32, shape, dim)


def ones_where(condition, dtype=BF16):
    return jnp.where(condition, 1.0, 0.0).astype(dtype)


def dot(left, right):
    return jnp.dot(left, right, preferred_element_type=F32)


def dot_rows(left, right):
    return lax.dot_general(left, right, (((1,), (1,)), ((), ())), preferred_element_type=F32)


def dot_columns(left, right):
    return lax.dot_general(left, right, (((0,), (0,)), ((), ())), preferred_element_type=F32)


def column_of(row):
    return jnp.transpose(jnp.broadcast_to(row, (LANES, LANES)))


def halves():
    return [slice(LANES * side, LANES * side + LANES) for side in range(WIDE // LANES)]


def build_tables(r):
    before, after = column_of(r.span[0:1]), column_of(r.span[1:2])
    for lag in range(1, 7):
        r.fore_short[lag - 1] = ones_where(before >= lag, F32)
        r.back_short[lag - 1] = ones_where(after >= lag, F32)
    taps = r.medium.shape[0]
    source = iota((taps, LANES), 0)
    lane = iota((taps, LANES), 1)
    filt = r.medium[...].astype(BF16)
    r.fore_rows[...] = dot_columns(filt, ones_where(lane == taps - source))
    r.back_rows[...] = dot_columns(filt, ones_where(lane == source))
    row = iota((HALF, LANES), 0)
    lane = iota((HALF, LANES), 1)
    for half in range(2):
        part = slice(HALF * half, HALF * half + HALF)
        lag = row + HALF - lane
        r.fore_mask[half] = ones_where((lag >= 0) & (lag < taps) & (lag <= before[part]))
        lag = lane - row
        back = (lag >= 0) & (lag < taps) & (lag <= after[part])
        r.back_mask[half] = ones_where(back)
        r.back_mask32[half] = ones_where(back, F32)
    live = r.lengths[0, 0] + r.lengths[0, 1]
    place = iota((TAIL_ROWS, r.cap), 0)
    column = iota((TAIL_ROWS, r.cap), 1)
    for part in range(3):
        step = place - REACH * part
        pick = (step >= 0) & (step < REACH) & (column == live - REACH + step)
        r.tail_pick[part] = ones_where(pick)


def widen_taps(r, chunk):
    groups = r.short.shape[2]
    owner = (chunk * WIDE + iota((groups, WIDE), 1)) // 16
    spread = ones_where(iota((groups, WIDE), 0) == owner)
    for part in range(3):
        r.taps[chunk, part, 0:7] = dot(r.short[part].astype(BF16), spread)


def tail_chunk(r, chunk):
    total = dot(r.tail_pick[0], r.raw[chunk, 0])
    for part in range(1, 3):
        total = total + dot(r.tail_pick[part], r.raw[chunk, part])
    r.tail_out[chunk] = total.astype(BF16).reshape(TAIL_ROWS // 16, 16, WIDE)


def build_picks(r, drift):
    live = r.lengths[0, 0] + r.lengths[0, 1]
    shape = (LEAD + COUNT, r.cap)
    token = iota(shape, 0) - LEAD - jnp.broadcast_to(drift, shape)
    column = iota(shape, 1)
    r.own_pick[...] = ones_where((column == token) & (column < live))
    shape = (LEAD + COUNT, LANES)
    token = iota(shape, 0) - LEAD - jnp.broadcast_to(drift, shape)
    column = iota(shape, 1)
    for part in range(3):
        late = token + REACH
        from_tail = (late >= 0) & (late < REACH) & (column == REACH * part + late)
        over = token - live
        from_head = (over >= 0) & (column == TAIL_ROWS + HEAD_ROWS * part + over)
        r.edge_pick[part] = ones_where(from_tail | from_head)


def strips(rows):
    return [slice(first, first + rows) for first in range(0, COUNT, rows)]


def filter_strip(r, chunk, part, lanes, window, masks):
    total = r.taps[chunk, part, 0:1, lanes] * window(0)
    for lag in range(1, 7):
        total = total + r.taps[chunk, part, lag : lag + 1, lanes] * (masks[lag - 1] * window(lag))
    return total


def forward_chunk(r, chunk):
    edges = r.edges[chunk].reshape(COUNT, WIDE)
    for part in range(3):
        packed = dot(r.own_pick[...], r.raw[chunk, part]) + dot(r.edge_pick[part], edges)
        for side, lanes in enumerate(halves()):
            r.rows[chunk, part, side] = packed[:, lanes]
    for side, lanes in enumerate(halves()):
        cot = jnp.transpose(r.cot[chunk, lanes].astype(F32))
        r.cot_rows[chunk, :, lanes] = cot
        for strip in strips(32):
            masks = [r.fore_short[lag, strip] for lag in range(6)]
            query, key, value = [
                filter_strip(
                    r,
                    chunk,
                    part,
                    lanes,
                    lambda lag: r.rows[chunk, part, side, LEAD + strip.start - lag : LEAD + strip.stop - lag],
                    masks,
                )
                for part in range(3)
            ]
            r.filtered[chunk, 0, strip, lanes] = key
            r.filtered[chunk, 1, strip, lanes] = value
            r.mixed[chunk, HALF + strip.start : HALF + strip.stop, lanes] = (key * value).astype(BF16)
            r.weighted[chunk, strip, lanes] = (cot[strip] * query).astype(BF16)


def toeplitz(rows, g):
    row = jnp.broadcast_to(rows[g : g + 1], (HALF, LANES)).astype(BF16)
    return pltpu.roll(row, 0, 1, stride=1, stride_axis=0)


def own_lanes(every, pair_of):
    result = every[:HALF]
    for pair in range(1, 4):
        result = jnp.where(pair_of == pair, every[HALF * pair : HALF * pair + HALF], result)
    return result


def paired(bands, mask):
    bands = [band * mask for band in bands]
    pairs = [jnp.concatenate(bands[2 * p : 2 * p + 2], axis=1) for p in range(4)]
    return jnp.concatenate(pairs, axis=0)


def medium_chunk(r, chunk):
    shape = (HALF + COUNT, LANES)
    even = iota(shape, 1) // 16 % 2 == 0
    pair_of = iota((HALF, LANES), 1) // 32
    for side, lanes in enumerate(halves()):
        first = pl.multiple_of(chunk * 16 + 8 * side, 8)
        fore = r.fore_rows[pl.ds(first, 8)]
        back = r.back_rows[pl.ds(first, 8)]
        fores = [toeplitz(fore, g) for g in range(8)]
        backs = [toeplitz(back, g) for g in range(8)]
        mixed = r.mixed[chunk, :, lanes]
        weighted = r.weighted[chunk, :, lanes]
        zero = jnp.zeros(shape, BF16)
        mixed_of = [jnp.where(even, mixed, zero), jnp.where(even, zero, mixed)]
        weighted_of = [jnp.where(even, weighted, zero), jnp.where(even, zero, weighted)]
        corr = [None] * 8
        for half in range(2):
            part = slice(HALF * half, HALF * half + HALF)
            window = slice(HALF * half, HALF * half + 2 * HALF)
            earlier = jnp.concatenate([m[window] for m in mixed_of], axis=0)
            later = jnp.concatenate([w[window] for w in weighted_of], axis=0)
            response = own_lanes(dot(paired(fores, r.fore_mask[half]), earlier), pair_of)
            spread = own_lanes(dot(paired(backs, r.back_mask[half]), later), pair_of)
            grads = (
                r.cot_rows[chunk, part, lanes] * response,
                spread * r.filtered[chunk, 1, part, lanes],
                spread * r.filtered[chunk, 0, part, lanes],
            )
            for b in range(3):
                grad = grads[b].astype(BF16)
                if half == 0:
                    r.grad_head[chunk, b, :, lanes] = grad[:HEAD_ROWS]
                r.grads[chunk, b, side, part] = grad.astype(F32)
            own = mixed[HALF + HALF * half : 2 * HALF + HALF * half]
            alone = [jnp.where(pair_of == p, own, zero[:HALF]) for p in range(4)]
            every = dot_rows(jnp.concatenate(alone, axis=0), later)
            mask = r.back_mask32[half]
            for g in range(8):
                tile = every[HALF * (g // 2) : HALF * (g // 2) + HALF]
                term = tile[:, LANES * (g % 2) : LANES * (g % 2) + LANES] * mask
                corr[g] = term if half == 0 else corr[g] + term
        for g in range(8):
            total = corr[g][0:8]
            for strip in range(1, 8):
                total = total + pltpu.roll(corr[g][8 * strip : 8 * strip + 8], LANES - 8 * strip, 1)
            r.corr[first + g] = total


def medium_sums(r):
    total = None
    for row in range(8):
        strip = r.corr[:, row, :]
        strip = strip if row == 0 else pltpu.roll(strip, LANES - row, 1)
        total = strip if total is None else total + strip
    total = jnp.transpose(total)
    for place in range(TEAM):
        strip, side = place // 2, place % 2
        r.sum_mine[place, 0:8] = total[8 * strip : 8 * strip + 8, LANES * side : LANES * side + LANES]


def short_sums_chunk(r, chunk):
    for side, lanes in enumerate(halves()):
        sums = [None] * 24
        for strip in strips(16):
            masks = [r.fore_short[lag, strip] for lag in range(6)]
            for part in range(3):
                grad = r.grads[chunk, part, side, strip]
                for lag in range(7):
                    window = r.rows[chunk, part, side, LEAD + strip.start - lag : LEAD + strip.stop - lag]
                    term = grad * window if lag == 0 else (masks[lag - 1] * grad) * window
                    term = term[0:8] + term[8:16]
                    place = 7 * part + lag
                    sums[place] = term if sums[place] is None else sums[place] + term
        for place in range(21):
            r.short_parts[(chunk * 2 + side) * 24 + place] = sums[place]


def short_sums(r):
    total = r.short_parts[:, 0, :]
    for row in range(1, 8):
        total = total + r.short_parts[:, row, :]
    gather = ones_where(iota((LANES, LANES), 1) == iota((LANES, LANES), 0) // 16)
    high = total.astype(BF16)
    low = (total - high.astype(F32)).astype(BF16)
    grouped = dot(high, gather) + dot(low, gather)
    for side in range(2):
        total = None
        for block in range(16):
            first = (16 * side + block) * 24
            strip = grouped[first : first + 24]
            strip = pltpu.roll(strip, 8 * block, 1) if block else strip
            total = strip if total is None else total + strip
        for place in range(side, TEAM, 2):
            r.sum_mine[place, 8:11] = total[3 * (place // 2) : 3 * (place // 2) + 3]


def backward_chunk(r, chunk):
    for side, lanes in enumerate(halves()):
        totals = [[], [], []]
        for part in range(3):
            r.grads[chunk, part, side, COUNT:] = r.grad_halo[chunk, part, :, lanes].astype(F32)
        for strip in strips(32):
            masks = [r.back_short[lag, strip] for lag in range(6)]
            for part in range(3):
                window = lambda lag: r.grads[chunk, part, side, strip.start + lag : strip.stop + lag]
                totals[part].append(filter_strip(r, chunk, part, lanes, window, masks))
        rows = pl.ds(pl.multiple_of(chunk * WIDE + LANES * side, LANES), LANES)
        for part in range(3):
            r.out[part, rows] = jnp.transpose(jnp.concatenate(totals[part], axis=0)).astype(BF16)


OPERANDS = ["lengths", "raw_hbm", "short", "medium", "span", "cot_hbm"]
RESULTS = ["out", "short_out", "medium_out"]


def scratch(cap, chunks, groups):
    vmem = pltpu.VMEM
    dma = pltpu.SemaphoreType.DMA
    return {
        "raw": vmem((chunks, 3, cap, WIDE), BF16),
        "cot": vmem((chunks, WIDE, COUNT), BF16),
        "tail_out": vmem((chunks, TAIL_ROWS // 16, 16, WIDE), BF16),
        "edges": vmem((chunks, 8, 16, WIDE), BF16),
        "own_pick": vmem((LEAD + COUNT, cap), BF16),
        "edge_pick": vmem((3, LEAD + COUNT, LANES), BF16),
        "tail_pick": vmem((3, TAIL_ROWS, cap), BF16),
        "fore_short": vmem((6, COUNT, LANES), F32),
        "back_short": vmem((6, COUNT, LANES), F32),
        "taps": vmem((chunks, 3, 8, WIDE), F32),
        "rows": vmem((chunks, 3, 2, LEAD + COUNT, LANES), F32),
        "filtered": vmem((chunks, 2, COUNT, WIDE), F32),
        "cot_rows": vmem((chunks, COUNT, WIDE), F32),
        "mixed": vmem((chunks, HALF + COUNT, WIDE), BF16),
        "weighted": vmem((chunks, COUNT + HALF, WIDE), BF16),
        "fore_rows": vmem((groups, LANES), F32),
        "back_rows": vmem((groups, LANES), F32),
        "fore_mask": vmem((2, HALF, LANES), BF16),
        "back_mask": vmem((2, HALF, LANES), BF16),
        "back_mask32": vmem((2, HALF, LANES), F32),
        "grads": vmem((chunks, 3, 2, COUNT + 16, LANES), F32),
        "grad_head": vmem((chunks, 3, HEAD_ROWS, WIDE), BF16),
        "grad_halo": vmem((chunks, 3, HEAD_ROWS, WIDE), BF16),
        "corr": vmem((groups, 8, LANES), F32),
        "short_parts": vmem((chunks * 2 * 24, 8, LANES), F32),
        "live_out": vmem((2, 8, LANES), I32),
        "live_near": vmem((INNER, 8, LANES), I32),
        "live_far": vmem((INNER, 8, LANES), I32),
        "sum_mine": vmem((TEAM, 11, LANES), F32),
        "sum_first": vmem((TEAM, 11, LANES), F32),
        "sum_second": vmem((TEAM, 11, LANES), F32),
        "sum_all": vmem((TEAM, 11, LANES), F32),
        "short_all": vmem((24, groups), F32),
        "load_sem": dma((2, chunks)),
        "send_sem": dma((5, chunks)),
        "recv_sem": dma((5, chunks)),
        "live_send": dma((2, INNER)),
        "live_recv": dma((2, INNER)),
        "sum_send": dma((3, TEAM)),
        "sum_recv": dma((3, TEAM)),
    }


def kernel(names, scale, *refs):
    r = types.SimpleNamespace(**dict(zip(names, refs)))
    r.cap = r.raw.shape[2]
    chunks = r.raw.shape[0]
    x, me = lax.axis_index("dp"), lax.axis_index("ctx")
    dp_count, ctx_count = lax.axis_size("dp"), lax.axis_size("ctx")
    right, left = lax.rem(me + 1, ctx_count), lax.rem(me + ctx_count - 1, ctx_count)
    row, col = lax.div(me, INNER), lax.rem(me, INNER)
    y, core = lax.div(col, 2), lax.rem(col, 2)
    place1, place2 = row * 2 + core, x * 4 + y

    def near_peer(hop):
        return {"ctx": row * INNER + lax.rem(col + hop, INNER)}

    def far_peer(hop):
        return {"ctx": lax.rem(row + hop, INNER) * INNER + col}

    def peer1(other):
        return {"dp": x, "ctx": lax.div(other, 2) * INNER + y * 2 + lax.rem(other, 2)}

    def peer2(other):
        return {"dp": lax.div(other, 4), "ctx": row * INNER + lax.rem(other, 4) * 2 + core}

    def remote(src, dst, send, recv, device):
        return pltpu.make_async_remote_copy(
            src, dst, send, recv, device_id=device, device_id_type=MESH
        )

    def load_raw(c):
        lanes = pl.ds(pl.multiple_of(c * WIDE, WIDE), WIDE)
        return pltpu.make_async_copy(r.raw_hbm.at[:, :, lanes], r.raw.at[c], r.load_sem.at[0, c])

    def load_cot(c):
        rows = pl.ds(pl.multiple_of(c * WIDE, WIDE), WIDE)
        return pltpu.make_async_copy(r.cot_hbm.at[rows], r.cot.at[c], r.load_sem.at[1, c])

    def send_tail(c):
        dst = r.edges.at[c, 0 : TAIL_ROWS // 16]
        return remote(r.tail_out.at[c], dst, r.send_sem.at[0, c], r.recv_sem.at[0, c], {"ctx": right})

    def send_head(c):
        src, dst = r.raw.at[c, :, 0:HEAD_ROWS], r.edges.at[c, TAIL_ROWS // 16 : 8]
        return remote(src, dst, r.send_sem.at[1, c], r.recv_sem.at[1, c], {"ctx": left})

    def send_mixed(c):
        src, dst = r.mixed.at[c, COUNT : COUNT + HALF], r.mixed.at[c, 0:HALF]
        return remote(src, dst, r.send_sem.at[2, c], r.recv_sem.at[2, c], {"ctx": right})

    def send_weighted(c):
        src, dst = r.weighted.at[c, 0:HALF], r.weighted.at[c, COUNT : COUNT + HALF]
        return remote(src, dst, r.send_sem.at[3, c], r.recv_sem.at[3, c], {"ctx": left})

    def send_grad(c):
        src, dst = r.grad_head.at[c], r.grad_halo.at[c]
        return remote(src, dst, r.send_sem.at[4, c], r.recv_sem.at[4, c], {"ctx": left})

    def live_copies(stage):
        near = stage == 0
        inbox = r.live_near if near else r.live_far
        return [
            remote(
                r.live_out.at[stage],
                inbox.at[INNER - hop],
                r.live_send.at[stage, hop],
                r.live_recv.at[stage, INNER - hop],
                near_peer(hop) if near else far_peer(hop),
            )
            for hop in range(1, INNER)
        ]

    def sum_copies(stage, source, target, peer, place):
        copies = []
        for hop in range(1, TEAM):
            other = lax.rem(place + hop, TEAM)
            copies.append(
                remote(
                    source(other),
                    target(TEAM - hop),
                    r.sum_send.at[stage, hop],
                    r.sum_recv.at[stage, TEAM - hop],
                    peer(other),
                )
            )
        return copies

    def start(copies):
        for copy in copies:
            copy.start()

    def finish(copies):
        for copy in copies:
            copy.wait()

    def each(step, first=0, last=chunks):
        def body(c, carry):
            step(c)
            return carry

        lax.fori_loop(first, last, body, 0)

    barrier = pltpu.get_barrier_semaphore()
    peers = [{"ctx": right}, {"ctx": left}]
    peers += [near_peer(hop) for hop in range(1, INNER)]
    peers += [far_peer(hop) for hop in range(1, INNER)]
    peers += [{"dp": lax.rem(x + hop, dp_count)} for hop in range(1, dp_count)]

    def loads(c):
        load_raw(c).start()

    each(loads)
    for peer in peers:
        pl.semaphore_signal(barrier, inc=1, device_id=peer, device_id_type=MESH)

    def cot_loads(c):
        load_cot(c).start()

    each(cot_loads)
    live = r.lengths[0, 0] + r.lengths[0, 1]
    r.live_out[0] = jnp.zeros((8, LANES), I32) + live
    build_tables(r)

    def tails(c):
        load_raw(c).wait()
        tail_chunk(r, c)

    each(tails, 0, chunks // 2)
    pl.semaphore_wait(barrier, len(peers))
    near = live_copies(0)
    start(near)

    def edges(c):
        send_tail(c).start()
        send_head(c).start()

    each(edges, 0, chunks // 2)
    finish(near)
    ahead = jnp.zeros((8, LANES), I32)
    whole = r.live_out[0]
    for hop in range(1, INNER):
        value = r.live_near[hop]
        whole = whole + value
        ahead = ahead + value * jnp.where(col + hop >= INNER, 1, 0)
    r.live_out[1] = whole
    far = live_copies(1)
    start(far)

    def tails_edges(c):
        tails(c)
        edges(c)

    each(tails_edges, chunks // 2, chunks)

    def widen(c):
        widen_taps(r, c)
        load_cot(c).wait()

    each(widen)
    finish(far)
    for hop in range(1, INNER):
        ahead = ahead + r.live_far[hop] * jnp.where(row + hop >= INNER, 1, 0)
    build_picks(r, ahead[0:1, 0:1] - me * COUNT)

    def forward(c):
        send_tail(c).wait_recv()
        send_head(c).wait_recv()
        forward_chunk(r, c)
        send_mixed(c).start()
        send_weighted(c).start()

    each(forward)

    def medium(c):
        send_mixed(c).wait_recv()
        send_weighted(c).wait_recv()
        medium_chunk(r, c)
        send_grad(c).start()
        short_sums_chunk(r, c)

    each(medium)
    medium_sums(r)
    short_sums(r)
    spread_out = sum_copies(
        0, lambda o: r.sum_mine.at[o], lambda h: r.sum_first.at[h], peer1, place1
    )
    start(spread_out)

    def backward(c):
        send_grad(c).wait_recv()
        backward_chunk(r, c)

    each(backward, 0, chunks * 3 // 8)
    finish(spread_out)
    total = r.sum_mine[place1]
    for hop in range(1, TEAM):
        total = total + r.sum_first[hop]
    r.sum_second[0] = total
    across = sum_copies(
        1, lambda o: r.sum_second.at[0], lambda h: r.sum_second.at[h], peer2, place2
    )
    start(across)
    each(backward, chunks * 3 // 8, chunks * 3 // 4)
    finish(across)
    total = jnp.zeros((11, LANES), F32)
    for other in range(TEAM):
        total = total + r.sum_second[lax.rem(other - place2 + TEAM, TEAM)]
    r.sum_all[place1] = total * (1.0 / scale)
    handed = sum_copies(
        2, lambda o: r.sum_all.at[place1], lambda h: r.sum_all.at[place1], peer1, place1
    )
    start(handed)
    each(backward, chunks * 3 // 4, chunks)
    finish(handed)
    for place in range(TEAM):
        strip, side = place // 2, place % 2
        lanes = slice(LANES * side, LANES * side + LANES)
        r.medium_out[8 * strip : 8 * strip + 8, lanes] = r.sum_all[place, 0:8]
        r.short_all[3 * strip : 3 * strip + 3, lanes] = r.sum_all[place, 8:11]
    for part in range(3):
        r.short_out[part] = r.short_all[7 * part : 7 * part + 7]

    def settle(c):
        for send in (send_tail, send_head, send_mixed, send_weighted, send_grad):
            send(c).wait_send()

    each(settle)


def shards(raw_qkv, block_lengths, short_filter, medium_filter, doc_span, cotangent):
    count = cotangent.shape[2]
    width = cotangent.shape[1]
    groups = medium_filter.shape[0]
    group_size = width // groups
    raw = jnp.transpose(raw_qkv[0], (0, 2, 1))
    short = jnp.transpose(short_filter, (0, 2, 1))
    filt = jnp.transpose(medium_filter)
    scale = math.sqrt(lax.axis_size("dp") * lax.axis_size("ctx") * count * group_size)
    space = scratch(raw.shape[1], width // WIDE, groups)
    vmem = pl.BlockSpec(memory_space=pltpu.VMEM)
    anywhere = pl.BlockSpec(memory_space=pl.ANY)
    out, short_sum, medium_sum = pl.pallas_call(
        functools.partial(kernel, OPERANDS + RESULTS + list(space), scale),
        in_specs=[pl.BlockSpec(memory_space=pltpu.SMEM), anywhere, vmem, vmem, vmem, anywhere],
        out_specs=[vmem, vmem, vmem],
        out_shape=[
            pltpu.VMEM((3, width, count), BF16),
            jax.ShapeDtypeStruct((3, 7, groups), F32),
            jax.ShapeDtypeStruct((64, groups), F32),
        ],
        scratch_shapes=list(space.values()),
        compiler_params=pltpu.CompilerParams(
            collective_id=0, has_side_effects=True, vmem_limit_bytes=56 * 1024 * 1024
        ),
    )(block_lengths[0], raw, short, filt, doc_span[0], cotangent[0])
    return (out[None], jnp.transpose(short_sum, (0, 2, 1)), jnp.transpose(medium_sum))


def solution(mesh):
    return jax.shard_map(
        shards,
        mesh=mesh,
        in_specs=(
            P("dp", None, None, "ctx"),
            P("dp", "ctx", None),
            P(),
            P(),
            P("dp", None, "ctx"),
            P("dp", None, "ctx"),
        ),
        out_specs=(P("dp", None, None, "ctx"), P(), P()),
        check_vma=False,
    )
```

time: 937 us -> 70.5 us (0.08)
  waiting for transfers between devices: 308 us -> 0 us
  local copies, waits for them, and re-layouts: 283 us -> 2.91 us
  other arithmetic: 171 us -> 0 us
  blocking collectives: 96.1 us -> 0 us
  Pallas kernels: 0 us -> 66.8 us
  matrix products: 35.7 us -> 0 us
  starting transfers between devices: 15.6 us -> 0 us
  between operations: 15.9 us -> 0.66 us
    psum x1 -> x0, waiting for transfers between devices: 302 us -> none  [shards(): short_sum, medium_sum = lax.psum((short_grad, medium_grad), ('dp', 'ctx'))]
    reshape x27 -> x0, local copies, waits for them, and re-layouts: 106 us -> none  [the longest x9 64.2 us: skewed(): tiled[..., :row_count * col_count]]
    psum x1 -> x0, blocking collectives: 76.4 us -> none  [shards(): short_sum, medium_sum = lax.psum((short_grad, medium_grad), ('dp', 'ctx'))]
    pallas_call x0 -> x1, Pallas kernels: none -> 66.8 us  [shards(): pl.pallas_call(functools.partial(kernel, OPERANDS + RESULTS + list(space)...]
    add x3 -> x0, other arithmetic: 45.1 us -> none  [the longest x2 45.1 us: short_pass(): summed = summed + jnp.where(tap_lag <= before, factor * window, 0.0)]
    dot_general x5 -> x0, matrix products: 35.7 us -> none  [the longest x2 12.5 us: block_out(): jnp.einsum('gct,gcu->gtu', left_op, right_op, preferred_element_type=jnp....]
    another operation x21 -> x0, local copies, waits for them, and re-layouts: 32.9 us -> none  [the longest x17 26.9 us: skewed(): tiled = jnp.tile(pattern, (1,) * len(lead_shape) + (row_count,))]
    reduce_sum x13 -> x0, other arithmetic: 32 us -> none  [the longest x2 23.7 us: shards(): jnp.sum(jnp.where(tap_lag <= before, grad_filtered.astype(jnp.float32) *...]
  transfers between devices with their start and end apart: 5 -> 0, of which waited for: 2 -> 0; matrix products, arithmetic and copies ran while one was open for 26% -> 0% of each run, Pallas kernels for 0% -> 0%
where the time goes in v2:
time: 70.5 us; the launch traced here: 70.4 us
  Pallas kernels  66.8 us (95%)
  local copies, waits for them, and re-layouts  2.91 us (4%)
    pallas_call x1, Pallas kernels, shards(): pl.pallas_call(functools.partial(kernel, OPERANDS + RESULTS + list(space)...  66.8 us
    unnamed x7, local copies, waits for them, and re-layouts  2.91 us

profile of v2, /device:TPU:1, one launch (start us, length us, event | category | flops | bytes accessed | tf_op | source)
XLA Modules:
  0.0 70.4 jit_solution(3815492413194896177)
XLA Ops:
  0.6 66.8 %shard_map.85 = (bf16[3,4096,128]{2,1,0:T(8,128)(2,1)S(1)}, f32[3,7,256]{2,1,0:T(8,128)}, f32[64,256]{1,0:T(8,128)}) custom-call(s32[1,2]{1,0:T(1,128)} %bitcast.19, bf16[3,160,4096]{2,1,0:T(8,128)(2,1)} %bitcast.12, f32[3,7,256]{2,1,0:T(8,128)} %bitcast.16, f32[64,256]{1,0:T(8,128)} %bitcast.14, s32[2,128]{1,0:T(2,128)} %bitcast.18, bf16[4096,128]{1,0:T(8,128)(2,1)} %bitcast.13), custom_call_target="tpu_custom_call" | custom-call | tf_op jit(solution)/shard_map/pallas_call | solution.py:576
  67.5 0.0 copy-start.1
  67.5 0.0 copy-start
  67.5 1.7 %copy.12 = bf16[1,3,4096,128]{3,2,1,0:T(8,128)(2,1)} copy(bf16[1,3,4096,128]{3,2,1,0:T(8,128)(2,1)S(1)} %bitcast.11) | data formatting | bytes 6291456
  69.2 0.0 copy-done.1
  69.2 0.6 copy.13
  69.8 0.0 copy-done
  69.8 0.6 copy.14
Async XLA Ops:
  67.5 1.7 %copy-start.1 = (f32[3,7,256]{2,1,0:T(8,128)S(1)}, f32[3,7,256]{2,1,0:T(8,128)}, u32[]{:S(2)}) copy-start(f32[3,7,256]{2,1,0:T(8,128)} %get-tuple-element.7) | copy-start | bytes 64516
  67.5 2.3 %copy-start = (f32[64,256]{1,0:T(8,128)S(1)}, f32[64,256]{1,0:T(8,128)}, u32[]{:S(2)}) copy-start(f32[64,256]{1,0:T(8,128)} %get-tuple-element.8) | copy-start | bytes 196612

commit v3 on v2

--- a/solution.py
+++ b/solution.py
@@ -35,10 +35,6 @@
 
 def dot(left, right):
     return jnp.dot(left, right, preferred_element_type=F32)
-
-
-def dot_rows(left, right):
-    return lax.dot_general(left, right, (((1,), (1,)), ((), ())), preferred_element_type=F32)
 
 
 def dot_columns(left, right):
@@ -84,11 +80,12 @@
 
 
 def widen_taps(r, chunk):
-    groups = r.short.shape[2]
-    owner = (chunk * WIDE + iota((groups, WIDE), 1)) // 16
-    spread = ones_where(iota((groups, WIDE), 0) == owner)
+    span = LANES * 16 // WIDE
+    owner = lax.rem(chunk, span) * (WIDE // 16) + iota((LANES, WIDE), 1) // 16
+    spread = ones_where(iota((LANES, WIDE), 0) == owner)
+    window = pl.ds(pl.multiple_of(lax.div(chunk, span) * LANES, LANES), LANES)
     for part in range(3):
-        r.taps[chunk, part, 0:7] = dot(r.short[part].astype(BF16), spread)
+        r.taps[chunk, part, 0:7] = dot(r.short[part, :, window].astype(BF16), spread)
 
 
 def tail_chunk(r, chunk):
@@ -207,7 +204,13 @@
                 r.grads[chunk, b, side, part] = grad.astype(F32)
             own = mixed[HALF + HALF * half : 2 * HALF + HALF * half]
             alone = [jnp.where(pair_of == p, own, zero[:HALF]) for p in range(4)]
-            every = dot_rows(jnp.concatenate(alone, axis=0), later)
+            turned = jnp.transpose(weighted[window])
+            blank = jnp.zeros((16, LANES), BF16)
+            sides = []
+            for parity in range(2):
+                blocks = [turned[16 * g : 16 * g + 16] if g % 2 == parity else blank for g in range(8)]
+                sides.append(jnp.concatenate(blocks, axis=0))
+            every = dot(jnp.concatenate(alone, axis=0), jnp.concatenate(sides, axis=1))
             mask = r.back_mask32[half]
             for g in range(8):
                 tile = every[HALF * (g // 2) : HALF * (g // 2) + HALF]
@@ -325,12 +328,12 @@
         "sum_all": vmem((TEAM, 11, LANES), F32),
         "short_all": vmem((24, groups), F32),
         "load_sem": dma((2, chunks)),
-        "send_sem": dma((5, chunks)),
+        "send_sem": dma((5,)),
         "recv_sem": dma((5, chunks)),
-        "live_send": dma((2, INNER)),
-        "live_recv": dma((2, INNER)),
-        "sum_send": dma((3, TEAM)),
-        "sum_recv": dma((3, TEAM)),
+        "live_send": dma((2,)),
+        "live_recv": dma((2,)),
+        "sum_send": dma((3,)),
+        "sum_recv": dma((3,)),
     }
 
 
@@ -372,23 +375,23 @@
 
     def send_tail(c):
         dst = r.edges.at[c, 0 : TAIL_ROWS // 16]
-        return remote(r.tail_out.at[c], dst, r.send_sem.at[0, c], r.recv_sem.at[0, c], {"ctx": right})
+        return remote(r.tail_out.at[c], dst, r.send_sem.at[0], r.recv_sem.at[0, c], {"ctx": right})
 
     def send_head(c):
         src, dst = r.raw.at[c, :, 0:HEAD_ROWS], r.edges.at[c, TAIL_ROWS // 16 : 8]
-        return remote(src, dst, r.send_sem.at[1, c], r.recv_sem.at[1, c], {"ctx": left})
+        return remote(src, dst, r.send_sem.at[1], r.recv_sem.at[1, c], {"ctx": left})
 
     def send_mixed(c):
         src, dst = r.mixed.at[c, COUNT : COUNT + HALF], r.mixed.at[c, 0:HALF]
-        return remote(src, dst, r.send_sem.at[2, c], r.recv_sem.at[2, c], {"ctx": right})
+        return remote(src, dst, r.send_sem.at[2], r.recv_sem.at[2, c], {"ctx": right})
 
     def send_weighted(c):
         src, dst = r.weighted.at[c, 0:HALF], r.weighted.at[c, COUNT : COUNT + HALF]
-        return remote(src, dst, r.send_sem.at[3, c], r.recv_sem.at[3, c], {"ctx": left})
+        return remote(src, dst, r.send_sem.at[3], r.recv_sem.at[3, c], {"ctx": left})
 
     def send_grad(c):
         src, dst = r.grad_head.at[c], r.grad_halo.at[c]
-        return remote(src, dst, r.send_sem.at[4, c], r.recv_sem.at[4, c], {"ctx": left})
+        return remote(src, dst, r.send_sem.at[4], r.recv_sem.at[4, c], {"ctx": left})
 
     def live_copies(stage):
         near = stage == 0
@@ -397,8 +400,8 @@
             remote(
                 r.live_out.at[stage],
                 inbox.at[INNER - hop],
-                r.live_send.at[stage, hop],
-                r.live_recv.at[stage, INNER - hop],
+                r.live_send.at[stage],
+                r.live_recv.at[stage],
                 near_peer(hop) if near else far_peer(hop),
             )
             for hop in range(1, INNER)
@@ -412,8 +415,8 @@
                 remote(
                     source(other),
                     target(TEAM - hop),
-                    r.sum_send.at[stage, hop],
-                    r.sum_recv.at[stage, TEAM - hop],
+                    r.sum_send.at[stage],
+                    r.sum_recv.at[stage],
                     peer(other),
                 )
             )
@@ -423,9 +426,18 @@
         for copy in copies:
             copy.start()
 
-    def finish(copies):
-        for copy in copies:
-            copy.wait()
+    def take(ref, sem):
+        pltpu.make_async_copy(ref, ref, sem).wait()
+
+    def finish_live(stage):
+        some = r.live_near.at[1:INNER]
+        take(some, r.live_send.at[stage])
+        take(some, r.live_recv.at[stage])
+
+    def finish_sum(stage):
+        some = r.sum_first.at[1:TEAM]
+        take(some, r.sum_send.at[stage])
+        take(some, r.sum_recv.at[stage])
 
     def each(step, first=0, last=chunks):
         def body(c, carry):
@@ -461,15 +473,14 @@
 
     each(tails, 0, chunks // 2)
     pl.semaphore_wait(barrier, len(peers))
-    near = live_copies(0)
-    start(near)
+    start(live_copies(0))
 
     def edges(c):
         send_tail(c).start()
         send_head(c).start()
 
     each(edges, 0, chunks // 2)
-    finish(near)
+    finish_live(0)
     ahead = jnp.zeros((8, LANES), I32)
     whole = r.live_out[0]
     for hop in range(1, INNER):
@@ -477,8 +488,7 @@
         whole = whole + value
         ahead = ahead + value * jnp.where(col + hop >= INNER, 1, 0)
     r.live_out[1] = whole
-    far = live_copies(1)
-    start(far)
+    start(live_copies(1))
 
     def tails_edges(c):
         tails(c)
@@ -491,7 +501,7 @@
         load_cot(c).wait()
 
     each(widen)
-    finish(far)
+    finish_live(1)
     for hop in range(1, INNER):
         ahead = ahead + r.live_far[hop] * jnp.where(row + hop >= INNER, 1, 0)
     build_picks(r, ahead[0:1, 0:1] - me * COUNT)
@@ -525,7 +535,7 @@
         backward_chunk(r, c)
 
     each(backward, 0, chunks * 3 // 8)
-    finish(spread_out)
+    finish_sum(0)
     total = r.sum_mine[place1]
     for hop in range(1, TEAM):
         total = total + r.sum_first[hop]
@@ -535,7 +545,7 @@
     )
     start(across)
     each(backward, chunks * 3 // 8, chunks * 3 // 4)
-    finish(across)
+    finish_sum(1)
     total = jnp.zeros((11, LANES), F32)
     for other in range(TEAM):
         total = total + r.sum_second[lax.rem(other - place2 + TEAM, TEAM)]
@@ -545,7 +555,7 @@
     )
     start(handed)
     each(backward, chunks * 3 // 4, chunks)
-    finish(handed)
+    finish_sum(2)
     for place in range(TEAM):
         strip, side = place // 2, place % 2
         lanes = slice(LANES * side, LANES * side + LANES)
@@ -554,11 +564,11 @@
     for part in range(3):
         r.short_out[part] = r.short_all[7 * part : 7 * part + 7]
 
-    def settle(c):
-        for send in (send_tail, send_head, send_mixed, send_weighted, send_grad):
-            send(c).wait_send()
-
-    each(settle)
+    take(r.tail_out, r.send_sem.at[0])
+    take(r.grad_head, r.send_sem.at[1])
+    take(r.mixed.at[:, 0:HALF], r.send_sem.at[2])
+    take(r.weighted.at[:, 0:HALF], r.send_sem.at[3])
+    take(r.grad_head, r.send_sem.at[4])
 
 
 def shards(raw_qkv, block_lengths, short_filter, medium_filter, doc_span, cotangent):

time: 70.5 us -> 67.9 us (0.963)
  Pallas kernels: 66.8 us -> 64.2 us
    pallas_call x1, Pallas kernels: 66.8 us -> 64.2 us  [shards(): pl.pallas_call(functools.partial(kernel, OPERANDS + RESULTS + list(space)...]
where the time goes in v3:
time: 67.9 us; the launch traced here: 67.8 us
  Pallas kernels  64.2 us (95%)
  local copies, waits for them, and re-layouts  2.91 us (4%)
    pallas_call x1, Pallas kernels, shards(): pl.pallas_call(functools.partial(kernel, OPERANDS + RESULTS + list(space)...  64.2 us
    unnamed x7, local copies, waits for them, and re-layouts  2.91 us

profile of v3, /device:TPU:1, one launch (start us, length us, event | category | flops | bytes accessed | tf_op | source)
XLA Modules:
  0.0 67.8 jit_solution(8063972947388401960)
XLA Ops:
  0.6 64.2 %shard_map.85 = (bf16[3,4096,128]{2,1,0:T(8,128)(2,1)S(1)}, f32[3,7,256]{2,1,0:T(8,128)}, f32[64,256]{1,0:T(8,128)}) custom-call(s32[1,2]{1,0:T(1,128)} %bitcast.19, bf16[3,160,4096]{2,1,0:T(8,128)(2,1)} %bitcast.12, f32[3,7,256]{2,1,0:T(8,128)} %bitcast.16, f32[64,256]{1,0:T(8,128)} %bitcast.14, s32[2,128]{1,0:T(2,128)} %bitcast.18, bf16[4096,128]{1,0:T(8,128)(2,1)} %bitcast.13), custom_call_target="tpu_custom_call" | custom-call | tf_op jit(solution)/shard_map/pallas_call | solution.py:586
  64.9 0.0 copy-start.1
  64.9 0.0 copy-start
  64.9 1.7 %copy.12 = bf16[1,3,4096,128]{3,2,1,0:T(8,128)(2,1)} copy(bf16[1,3,4096,128]{3,2,1,0:T(8,128)(2,1)S(1)} %bitcast.11) | data formatting | bytes 6291456
  66.5 0.0 copy-done.1
  66.5 0.6 copy.13
  67.2 0.0 copy-done
  67.2 0.6 copy.14
Async XLA Ops:
  64.9 1.7 %copy-start.1 = (f32[3,7,256]{2,1,0:T(8,128)S(1)}, f32[3,7,256]{2,1,0:T(8,128)}, u32[]{:S(2)}) copy-start(f32[3,7,256]{2,1,0:T(8,128)} %get-tuple-element.7) | copy-start | bytes 64516
  64.9 2.3 %copy-start = (f32[64,256]{1,0:T(8,128)S(1)}, f32[64,256]{1,0:T(8,128)}, u32[]{:S(2)}) copy-start(f32[64,256]{1,0:T(8,128)} %get-tuple-element.8) | copy-start | bytes 196612

commit v4 on v3

--- a/solution.py
+++ b/solution.py
@@ -123,6 +123,11 @@
     return total
 
 
+def turn_chunk(r, chunk):
+    for lanes in halves():
+        r.cot_rows[chunk, :, lanes] = jnp.transpose(r.cot[chunk, lanes].astype(F32))
+
+
 def forward_chunk(r, chunk):
     edges = r.edges[chunk].reshape(COUNT, WIDE)
     for part in range(3):
@@ -130,8 +135,6 @@
         for side, lanes in enumerate(halves()):
             r.rows[chunk, part, side] = packed[:, lanes]
     for side, lanes in enumerate(halves()):
-        cot = jnp.transpose(r.cot[chunk, lanes].astype(F32))
-        r.cot_rows[chunk, :, lanes] = cot
         for strip in strips(32):
             masks = [r.fore_short[lag, strip] for lag in range(6)]
             query, key, value = [
@@ -148,7 +151,7 @@
             r.filtered[chunk, 0, strip, lanes] = key
             r.filtered[chunk, 1, strip, lanes] = value
             r.mixed[chunk, HALF + strip.start : HALF + strip.stop, lanes] = (key * value).astype(BF16)
-            r.weighted[chunk, strip, lanes] = (cot[strip] * query).astype(BF16)
+            r.weighted[chunk, strip, lanes] = (r.cot_rows[chunk, strip, lanes] * query).astype(BF16)
 
 
 def toeplitz(rows, g):
@@ -167,6 +170,18 @@
     bands = [band * mask for band in bands]
     pairs = [jnp.concatenate(bands[2 * p : 2 * p + 2], axis=1) for p in range(4)]
     return jnp.concatenate(pairs, axis=0)
+
+
+def bands_chunk(r, chunk):
+    for side in range(2):
+        first = pl.multiple_of(chunk * 16 + 8 * side, 8)
+        fore = r.fore_rows[pl.ds(first, 8)]
+        back = r.back_rows[pl.ds(first, 8)]
+        fores = [toeplitz(fore, g) for g in range(8)]
+        backs = [toeplitz(back, g) for g in range(8)]
+        for half in range(2):
+            r.fore_bands[chunk, side, half] = paired(fores, r.fore_mask[half])
+            r.back_bands[chunk, side, half] = paired(backs, r.back_mask[half])
 
 
 def medium_chunk(r, chunk):
@@ -175,10 +190,6 @@
     pair_of = iota((HALF, LANES), 1) // 32
     for side, lanes in enumerate(halves()):
         first = pl.multiple_of(chunk * 16 + 8 * side, 8)
-        fore = r.fore_rows[pl.ds(first, 8)]
-        back = r.back_rows[pl.ds(first, 8)]
-        fores = [toeplitz(fore, g) for g in range(8)]
-        backs = [toeplitz(back, g) for g in range(8)]
         mixed = r.mixed[chunk, :, lanes]
         weighted = r.weighted[chunk, :, lanes]
         zero = jnp.zeros(shape, BF16)
@@ -190,8 +201,8 @@
             window = slice(HALF * half, HALF * half + 2 * HALF)
             earlier = jnp.concatenate([m[window] for m in mixed_of], axis=0)
             later = jnp.concatenate([w[window] for w in weighted_of], axis=0)
-            response = own_lanes(dot(paired(fores, r.fore_mask[half]), earlier), pair_of)
-            spread = own_lanes(dot(paired(backs, r.back_mask[half]), later), pair_of)
+            response = own_lanes(dot(r.fore_bands[chunk, side, half], earlier), pair_of)
+            spread = own_lanes(dot(r.back_bands[chunk, side, half], later), pair_of)
             grads = (
                 r.cot_rows[chunk, part, lanes] * response,
                 spread * r.filtered[chunk, 1, part, lanes],
@@ -253,9 +264,7 @@
 
 
 def short_sums(r):
-    total = r.short_parts[:, 0, :]
-    for row in range(1, 8):
-        total = total + r.short_parts[:, row, :]
+    total = jnp.sum(r.short_parts[...], axis=1)
     gather = ones_where(iota((LANES, LANES), 1) == iota((LANES, LANES), 0) // 16)
     high = total.astype(BF16)
     low = (total - high.astype(F32)).astype(BF16)
@@ -317,6 +326,8 @@
         "grads": vmem((chunks, 3, 2, COUNT + 16, LANES), F32),
         "grad_head": vmem((chunks, 3, HEAD_ROWS, WIDE), BF16),
         "grad_halo": vmem((chunks, 3, HEAD_ROWS, WIDE), BF16),
+        "fore_bands": vmem((chunks, 2, 2, 4 * HALF, 4 * HALF), BF16),
+        "back_bands": vmem((chunks, 2, 2, 4 * HALF, 4 * HALF), BF16),
         "corr": vmem((groups, 8, LANES), F32),
         "short_parts": vmem((chunks * 2 * 24, 8, LANES), F32),
         "live_out": vmem((2, 8, LANES), I32),
@@ -471,7 +482,11 @@
         load_raw(c).wait()
         tail_chunk(r, c)
 
-    each(tails, 0, chunks // 2)
+    def widen(c):
+        widen_taps(r, c)
+
+    each(tails)
+    each(widen)
     pl.semaphore_wait(barrier, len(peers))
     start(live_copies(0))
 
@@ -479,7 +494,14 @@
         send_tail(c).start()
         send_head(c).start()
 
-    each(edges, 0, chunks // 2)
+    each(edges)
+
+    def bands(c):
+        load_cot(c).wait()
+        turn_chunk(r, c)
+        bands_chunk(r, c)
+
+    each(bands, 0, chunks // 2)
     finish_live(0)
     ahead = jnp.zeros((8, LANES), I32)
     whole = r.live_out[0]
@@ -490,17 +512,7 @@
     r.live_out[1] = whole
     start(live_copies(1))
 
-    def tails_edges(c):
-        tails(c)
-        edges(c)
-
-    each(tails_edges, chunks // 2, chunks)
-
-    def widen(c):
-        widen_taps(r, c)
-        load_cot(c).wait()
-
-    each(widen)
+    each(bands, chunks // 2, chunks)
     finish_live(1)
     for hop in range(1, INNER):
         ahead = ahead + r.live_far[hop] * jnp.where(row + hop >= INNER, 1, 0)

time: 67.9 us -> 73.3 us (1.080)
  Pallas kernels: 64.2 us -> 69.6 us
    pallas_call x1, Pallas kernels: 64.2 us -> 69.6 us  [shards(): pl.pallas_call(functools.partial(kernel, OPERANDS + RESULTS + list(space)...]
where the time goes in v4:
time: 73.3 us; the launch traced here: 73.2 us
  Pallas kernels  69.6 us (95%)
  local copies, waits for them, and re-layouts  2.91 us (4%)
    pallas_call x1, Pallas kernels, shards(): pl.pallas_call(functools.partial(kernel, OPERANDS + RESULTS + list(space)...  69.6 us
    unnamed x7, local copies, waits for them, and re-layouts  2.91 us

profile of v4, /device:TPU:1, one launch (start us, length us, event | category | flops | bytes accessed | tf_op | source)
XLA Modules:
  0.0 73.2 jit_solution(5172875397055720629)
XLA Ops:
  0.6 69.6 %shard_map.85 = (bf16[3,4096,128]{2,1,0:T(8,128)(2,1)S(1)}, f32[3,7,256]{2,1,0:T(8,128)}, f32[64,256]{1,0:T(8,128)}) custom-call(s32[1,2]{1,0:T(1,128)} %bitcast.19, bf16[3,160,4096]{2,1,0:T(8,128)(2,1)} %bitcast.12, f32[3,7,256]{2,1,0:T(8,128)} %bitcast.16, f32[64,256]{1,0:T(8,128)} %bitcast.14, s32[2,128]{1,0:T(2,128)} %bitcast.18, bf16[4096,128]{1,0:T(8,128)(2,1)} %bitcast.13), custom_call_target="tpu_custom_call" | custom-call | tf_op jit(solution)/shard_map/pallas_call | solution.py:598
  70.3 0.0 copy-start.1
  70.3 0.0 copy-start
  70.3 1.7 %copy.12 = bf16[1,3,4096,128]{3,2,1,0:T(8,128)(2,1)} copy(bf16[1,3,4096,128]{3,2,1,0:T(8,128)(2,1)S(1)} %bitcast.11) | data formatting | bytes 6291456
  71.9 0.0 copy-done.1
  71.9 0.6 copy.13
  72.6 0.0 copy-done
  72.6 0.6 copy.14
Async XLA Ops:
  70.3 1.7 %copy-start.1 = (f32[3,7,256]{2,1,0:T(8,128)S(1)}, f32[3,7,256]{2,1,0:T(8,128)}, u32[]{:S(2)}) copy-start(f32[3,7,256]{2,1,0:T(8,128)} %get-tuple-element.7) | copy-start | bytes 64516
  70.3 2.3 %copy-start = (f32[64,256]{1,0:T(8,128)S(1)}, f32[64,256]{1,0:T(8,128)}, u32[]{:S(2)}) copy-start(f32[64,256]{1,0:T(8,128)} %get-tuple-element.8) | copy-start | bytes 196612

commit v5 on v3

--- a/solution.py
+++ b/solution.py
@@ -15,11 +15,14 @@
 MESH = pl.DeviceIdType.MESH
 LANES = 128
 WIDE = 256
+LATE = 64
 REACH = 22
 TAIL_ROWS = 80
 HEAD_ROWS = 16
 LEAD = 8
 HALF = 64
+FIRST_ROWS = 24
+LAST_ROWS = 16
 COUNT = 128
 TEAM = 16
 INNER = 8
@@ -47,6 +50,19 @@
 
 def halves():
     return [slice(LANES * side, LANES * side + LANES) for side in range(WIDE // LANES)]
+
+
+def build_tail_pick(r):
+    live = r.lengths[0, 0] + r.lengths[0, 1]
+    rows = r.cap - LATE
+    shape = (TAIL_ROWS, 3 * rows)
+    place, column = iota(shape, 0), iota(shape, 1)
+    pick = None
+    for part in range(3):
+        step = place - REACH * part
+        own = (step >= 0) & (step < REACH) & (column - rows * part == live - REACH + step - LATE)
+        pick = own if pick is None else pick | own
+    r.tail_pick[...] = ones_where(pick)
 
 
 def build_tables(r):
@@ -70,13 +86,6 @@
         back = (lag >= 0) & (lag < taps) & (lag <= after[part])
         r.back_mask[half] = ones_where(back)
         r.back_mask32[half] = ones_where(back, F32)
-    live = r.lengths[0, 0] + r.lengths[0, 1]
-    place = iota((TAIL_ROWS, r.cap), 0)
-    column = iota((TAIL_ROWS, r.cap), 1)
-    for part in range(3):
-        step = place - REACH * part
-        pick = (step >= 0) & (step < REACH) & (column == live - REACH + step)
-        r.tail_pick[part] = ones_where(pick)
 
 
 def widen_taps(r, chunk):
@@ -84,14 +93,15 @@
     owner = lax.rem(chunk, span) * (WIDE // 16) + iota((LANES, WIDE), 1) // 16
     spread = ones_where(iota((LANES, WIDE), 0) == owner)
     window = pl.ds(pl.multiple_of(lax.div(chunk, span) * LANES, LANES), LANES)
+    blank = jnp.zeros((1, LANES), F32)
+    taps = [row for part in range(3) for row in (r.short[part, :, window], blank)]
+    wide = dot(jnp.concatenate(taps, axis=0).astype(BF16), spread)
     for part in range(3):
-        r.taps[chunk, part, 0:7] = dot(r.short[part, :, window].astype(BF16), spread)
+        r.taps[chunk, part] = wide[8 * part : 8 * part + 8]
 
 
 def tail_chunk(r, chunk):
-    total = dot(r.tail_pick[0], r.raw[chunk, 0])
-    for part in range(1, 3):
-        total = total + dot(r.tail_pick[part], r.raw[chunk, part])
+    total = dot(r.tail_pick[...], r.raw[chunk, :, LATE:].reshape(3 * (r.cap - LATE), WIDE))
     r.tail_out[chunk] = total.astype(BF16).reshape(TAIL_ROWS // 16, 16, WIDE)
 
 
@@ -101,15 +111,21 @@
     token = iota(shape, 0) - LEAD - jnp.broadcast_to(drift, shape)
     column = iota(shape, 1)
     r.own_pick[...] = ones_where((column == token) & (column < live))
-    shape = (LEAD + COUNT, LANES)
+    shape = (FIRST_ROWS, LANES)
     token = iota(shape, 0) - LEAD - jnp.broadcast_to(drift, shape)
     column = iota(shape, 1)
     for part in range(3):
         late = token + REACH
         from_tail = (late >= 0) & (late < REACH) & (column == REACH * part + late)
+        r.edge_pick[FIRST_ROWS * part : FIRST_ROWS * part + FIRST_ROWS] = ones_where(from_tail, F32)
+    shape = (LAST_ROWS, LANES)
+    token = iota(shape, 0) + COUNT - LAST_ROWS - jnp.broadcast_to(drift, shape)
+    column = iota(shape, 1)
+    for part in range(3):
         over = token - live
         from_head = (over >= 0) & (column == TAIL_ROWS + HEAD_ROWS * part + over)
-        r.edge_pick[part] = ones_where(from_tail | from_head)
+        first = 3 * FIRST_ROWS + LAST_ROWS * part
+        r.edge_pick[first : first + LAST_ROWS] = ones_where(from_head, F32)
 
 
 def strips(rows):
@@ -124,11 +140,17 @@
 
 
 def forward_chunk(r, chunk):
-    edges = r.edges[chunk].reshape(COUNT, WIDE)
+    edges = dot(r.edge_pick[...].astype(BF16), r.edges[chunk].reshape(COUNT, WIDE))
     for part in range(3):
-        packed = dot(r.own_pick[...], r.raw[chunk, part]) + dot(r.edge_pick[part], edges)
+        packed = dot(r.own_pick[...], r.raw[chunk, part])
+        first = packed[:FIRST_ROWS] + edges[FIRST_ROWS * part : FIRST_ROWS * part + FIRST_ROWS]
+        place = 3 * FIRST_ROWS + LAST_ROWS * part
+        last = packed[LEAD + COUNT - LAST_ROWS :] + edges[place : place + LAST_ROWS]
+        middle = packed[FIRST_ROWS : LEAD + COUNT - LAST_ROWS]
         for side, lanes in enumerate(halves()):
-            r.rows[chunk, part, side] = packed[:, lanes]
+            r.rows[chunk, part, side, :FIRST_ROWS] = first[:, lanes]
+            r.rows[chunk, part, side, FIRST_ROWS : LEAD + COUNT - LAST_ROWS] = middle[:, lanes]
+            r.rows[chunk, part, side, LEAD + COUNT - LAST_ROWS :] = last[:, lanes]
     for side, lanes in enumerate(halves()):
         cot = jnp.transpose(r.cot[chunk, lanes].astype(F32))
         r.cot_rows[chunk, :, lanes] = cot
@@ -253,9 +275,7 @@
 
 
 def short_sums(r):
-    total = r.short_parts[:, 0, :]
-    for row in range(1, 8):
-        total = total + r.short_parts[:, row, :]
+    total = jnp.sum(r.short_parts[...], axis=1)
     gather = ones_where(iota((LANES, LANES), 1) == iota((LANES, LANES), 0) // 16)
     high = total.astype(BF16)
     low = (total - high.astype(F32)).astype(BF16)
@@ -299,8 +319,8 @@
         "tail_out": vmem((chunks, TAIL_ROWS // 16, 16, WIDE), BF16),
         "edges": vmem((chunks, 8, 16, WIDE), BF16),
         "own_pick": vmem((LEAD + COUNT, cap), BF16),
-        "edge_pick": vmem((3, LEAD + COUNT, LANES), BF16),
-        "tail_pick": vmem((3, TAIL_ROWS, cap), BF16),
+        "edge_pick": vmem((3 * (FIRST_ROWS + LAST_ROWS), LANES), F32),
+        "tail_pick": vmem((TAIL_ROWS, 3 * (cap - LATE)), BF16),
         "fore_short": vmem((6, COUNT, LANES), F32),
         "back_short": vmem((6, COUNT, LANES), F32),
         "taps": vmem((chunks, 3, 8, WIDE), F32),
@@ -465,21 +485,20 @@
     each(cot_loads)
     live = r.lengths[0, 0] + r.lengths[0, 1]
     r.live_out[0] = jnp.zeros((8, LANES), I32) + live
-    build_tables(r)
-
-    def tails(c):
-        load_raw(c).wait()
-        tail_chunk(r, c)
-
-    each(tails, 0, chunks // 2)
+    build_tail_pick(r)
     pl.semaphore_wait(barrier, len(peers))
     start(live_copies(0))
 
     def edges(c):
-        send_tail(c).start()
-        send_head(c).start()
-
-    each(edges, 0, chunks // 2)
+        for k in range(2):
+            load_raw(2 * c + k).wait()
+            send_head(2 * c + k).start()
+        for k in range(2):
+            tail_chunk(r, 2 * c + k)
+        for k in range(2):
+            send_tail(2 * c + k).start()
+
+    each(edges, 0, chunks // 4)
     finish_live(0)
     ahead = jnp.zeros((8, LANES), I32)
     whole = r.live_out[0]
@@ -490,17 +509,16 @@
     r.live_out[1] = whole
     start(live_copies(1))
 
-    def tails_edges(c):
-        tails(c)
-        edges(c)
-
-    each(tails_edges, chunks // 2, chunks)
+    each(edges, chunks // 4, chunks // 2)
+    build_tables(r)
 
     def widen(c):
-        widen_taps(r, c)
-        load_cot(c).wait()
-
-    each(widen)
+        for k in range(4):
+            widen_taps(r, 4 * c + k)
+        for k in range(4):
+            load_cot(4 * c + k).wait()
+
+    each(widen, 0, chunks // 4)
     finish_live(1)
     for hop in range(1, INNER):
         ahead = ahead + r.live_far[hop] * jnp.where(row + hop >= INNER, 1, 0)

time: 67.9 us -> 66.5 us (0.979)
  Pallas kernels: 64.2 us -> 62.8 us
    pallas_call x1, Pallas kernels: 64.2 us -> 62.8 us  [shards(): pl.pallas_call(functools.partial(kernel, OPERANDS + RESULTS + list(space)...]
where the time goes in v5:
time: 66.5 us; the launch traced here: 66.4 us
  Pallas kernels  62.8 us (94%)
  local copies, waits for them, and re-layouts  2.91 us (4%)
    pallas_call x1, Pallas kernels, shards(): pl.pallas_call(functools.partial(kernel, OPERANDS + RESULTS + list(space)...  62.8 us
    unnamed x7, local copies, waits for them, and re-layouts  2.91 us

profile of v5, /device:TPU:1, one launch (start us, length us, event | category | flops | bytes accessed | tf_op | source)
XLA Modules:
  0.0 66.4 jit_solution(3468692604516012474)
XLA Ops:
  0.6 62.8 %shard_map.85 = (bf16[3,4096,128]{2,1,0:T(8,128)(2,1)S(1)}, f32[3,7,256]{2,1,0:T(8,128)}, f32[64,256]{1,0:T(8,128)}) custom-call(s32[1,2]{1,0:T(1,128)} %bitcast.19, bf16[3,160,4096]{2,1,0:T(8,128)(2,1)} %bitcast.12, f32[3,7,256]{2,1,0:T(8,128)} %bitcast.16, f32[64,256]{1,0:T(8,128)} %bitcast.14, s32[2,128]{1,0:T(2,128)} %bitcast.18, bf16[4096,128]{1,0:T(8,128)(2,1)} %bitcast.13), custom_call_target="tpu_custom_call" | custom-call | tf_op jit(solution)/shard_map/pallas_call | solution.py:604
  63.5 0.0 copy-start.1
  63.5 0.0 copy-start
  63.5 1.7 %copy.12 = bf16[1,3,4096,128]{3,2,1,0:T(8,128)(2,1)} copy(bf16[1,3,4096,128]{3,2,1,0:T(8,128)(2,1)S(1)} %bitcast.11) | data formatting | bytes 6291456
  65.1 0.0 copy-done.1
  65.1 0.6 copy.13
  65.8 0.0 copy-done
  65.8 0.6 copy.14
Async XLA Ops:
  63.5 1.7 %copy-start.1 = (f32[3,7,256]{2,1,0:T(8,128)S(1)}, f32[3,7,256]{2,1,0:T(8,128)}, u32[]{:S(2)}) copy-start(f32[3,7,256]{2,1,0:T(8,128)} %get-tuple-element.7) | copy-start | bytes 64516
  63.5 2.3 %copy-start = (f32[64,256]{1,0:T(8,128)S(1)}, f32[64,256]{1,0:T(8,128)}, u32[]{:S(2)}) copy-start(f32[64,256]{1,0:T(8,128)} %get-tuple-element.8) | copy-start | bytes 196612

commit v6 on v5

--- a/solution.py
+++ b/solution.py
@@ -152,7 +152,7 @@
             r.rows[chunk, part, side, FIRST_ROWS : LEAD + COUNT - LAST_ROWS] = middle[:, lanes]
             r.rows[chunk, part, side, LEAD + COUNT - LAST_ROWS :] = last[:, lanes]
     for side, lanes in enumerate(halves()):
-        cot = jnp.transpose(r.cot[chunk, lanes].astype(F32))
+        cot = jnp.transpose(r.cot[chunk, lanes]).astype(F32)
         r.cot_rows[chunk, :, lanes] = cot
         for strip in strips(32):
             masks = [r.fore_short[lag, strip] for lag in range(6)]
@@ -219,10 +219,11 @@
                 spread * r.filtered[chunk, 1, part, lanes],
                 spread * r.filtered[chunk, 0, part, lanes],
             )
+            if half == 0:
+                heads = [grad[:8] for grad in grads] + [jnp.zeros((8, LANES), F32)]
+                r.grad_head[chunk, :, lanes] = jnp.concatenate(heads, axis=0).astype(BF16)
             for b in range(3):
                 grad = grads[b].astype(BF16)
-                if half == 0:
-                    r.grad_head[chunk, b, :, lanes] = grad[:HEAD_ROWS]
                 r.grads[chunk, b, side, part] = grad.astype(F32)
             own = mixed[HALF + HALF * half : 2 * HALF + HALF * half]
             alone = [jnp.where(pair_of == p, own, zero[:HALF]) for p in range(4)]
@@ -294,8 +295,9 @@
 def backward_chunk(r, chunk):
     for side, lanes in enumerate(halves()):
         totals = [[], [], []]
+        halo = r.grad_halo[chunk, :, lanes].astype(F32)
         for part in range(3):
-            r.grads[chunk, part, side, COUNT:] = r.grad_halo[chunk, part, :, lanes].astype(F32)
+            r.grads[chunk, part, side, COUNT : COUNT + 8] = halo[8 * part : 8 * part + 8]
         for strip in strips(32):
             masks = [r.back_short[lag, strip] for lag in range(6)]
             for part in range(3):
@@ -303,7 +305,7 @@
                 totals[part].append(filter_strip(r, chunk, part, lanes, window, masks))
         rows = pl.ds(pl.multiple_of(chunk * WIDE + LANES * side, LANES), LANES)
         for part in range(3):
-            r.out[part, rows] = jnp.transpose(jnp.concatenate(totals[part], axis=0)).astype(BF16)
+            r.out[part, rows] = jnp.transpose(jnp.concatenate(totals[part], axis=0).astype(BF16))
 
 
 OPERANDS = ["lengths", "raw_hbm", "short", "medium", "span", "cot_hbm"]
@@ -335,8 +337,8 @@
         "back_mask": vmem((2, HALF, LANES), BF16),
         "back_mask32": vmem((2, HALF, LANES), F32),
         "grads": vmem((chunks, 3, 2, COUNT + 16, LANES), F32),
-        "grad_head": vmem((chunks, 3, HEAD_ROWS, WIDE), BF16),
-        "grad_halo": vmem((chunks, 3, HEAD_ROWS, WIDE), BF16),
+        "grad_head": vmem((chunks, 32, WIDE), BF16),
+        "grad_halo": vmem((chunks, 32, WIDE), BF16),
         "corr": vmem((groups, 8, LANES), F32),
         "short_parts": vmem((chunks * 2 * 24, 8, LANES), F32),
         "live_out": vmem((2, 8, LANES), I32),
@@ -583,7 +585,7 @@
         r.short_out[part] = r.short_all[7 * part : 7 * part + 7]
 
     take(r.tail_out, r.send_sem.at[0])
-    take(r.grad_head, r.send_sem.at[1])
+    take(r.edges.at[:, TAIL_ROWS // 16 : 8], r.send_sem.at[1])
     take(r.mixed.at[:, 0:HALF], r.send_sem.at[2])
     take(r.weighted.at[:, 0:HALF], r.send_sem.at[3])
     take(r.grad_head, r.send_sem.at[4])

time: 66.5 us -> 65.9 us (level)
  no operation moved by 1% of the time
where the time goes in v6:
time: 65.9 us; the launch traced here: 65.8 us
  Pallas kernels  62.2 us (94%)
  local copies, waits for them, and re-layouts  2.91 us (4%)
  between operations  0.66 us (1%)
    pallas_call x1, Pallas kernels, shards(): pl.pallas_call(functools.partial(kernel, OPERANDS + RESULTS + list(space)...  62.2 us
    unnamed x7, local copies, waits for them, and re-layouts  2.91 us

profile of v6, /device:TPU:1, one launch (start us, length us, event | category | flops | bytes accessed | tf_op | source)
XLA Modules:
  0.0 65.8 jit_solution(16897714894223645638)
XLA Ops:
  0.6 62.2 %shard_map.85 = (bf16[3,4096,128]{2,1,0:T(8,128)(2,1)S(1)}, f32[3,7,256]{2,1,0:T(8,128)}, f32[64,256]{1,0:T(8,128)}) custom-call(s32[1,2]{1,0:T(1,128)} %bitcast.19, bf16[3,160,4096]{2,1,0:T(8,128)(2,1)} %bitcast.12, f32[3,7,256]{2,1,0:T(8,128)} %bitcast.16, f32[64,256]{1,0:T(8,128)} %bitcast.14, s32[2,128]{1,0:T(2,128)} %bitcast.18, bf16[4096,128]{1,0:T(8,128)(2,1)} %bitcast.13), custom_call_target="tpu_custom_call" | custom-call | tf_op jit(solution)/shard_map/pallas_call | solution.py:606
  62.8 0.0 copy-start.1
  62.8 0.0 copy-start
  62.8 1.7 %copy.12 = bf16[1,3,4096,128]{3,2,1,0:T(8,128)(2,1)} copy(bf16[1,3,4096,128]{3,2,1,0:T(8,128)(2,1)S(1)} %bitcast.11) | data formatting | bytes 6291456
  64.5 0.0 copy-done.1
  64.5 0.6 copy.13
  65.1 0.0 copy-done
  65.1 0.6 copy.14
Async XLA Ops:
  62.8 1.7 %copy-start.1 = (f32[3,7,256]{2,1,0:T(8,128)S(1)}, f32[3,7,256]{2,1,0:T(8,128)}, u32[]{:S(2)}) copy-start(f32[3,7,256]{2,1,0:T(8,128)} %get-tuple-element.7) | copy-start | bytes 64516
  62.8 2.3 %copy-start = (f32[64,256]{1,0:T(8,128)S(1)}, f32[64,256]{1,0:T(8,128)}, u32[]{:S(2)}) copy-start(f32[64,256]{1,0:T(8,128)} %get-tuple-element.8) | copy-start | bytes 196612

commit v7 on v6

--- a/solution.py
+++ b/solution.py
@@ -457,9 +457,7 @@
         take(some, r.live_recv.at[stage])
 
     def finish_sum(stage):
-        some = r.sum_first.at[1:TEAM]
-        take(some, r.sum_send.at[stage])
-        take(some, r.sum_recv.at[stage])
+        take(r.sum_first.at[1:TEAM], r.sum_recv.at[stage])
 
     def each(step, first=0, last=chunks):
         def body(c, carry):
@@ -554,7 +552,7 @@
         send_grad(c).wait_recv()
         backward_chunk(r, c)
 
-    each(backward, 0, chunks * 3 // 8)
+    each(backward, 0, chunks * 5 // 16)
     finish_sum(0)
     total = r.sum_mine[place1]
     for hop in range(1, TEAM):
@@ -564,7 +562,7 @@
         1, lambda o: r.sum_second.at[0], lambda h: r.sum_second.at[h], peer2, place2
     )
     start(across)
-    each(backward, chunks * 3 // 8, chunks * 3 // 4)
+    each(backward, chunks * 5 // 16, chunks * 5 // 8)
     finish_sum(1)
     total = jnp.zeros((11, LANES), F32)
     for other in range(TEAM):
@@ -574,7 +572,7 @@
         2, lambda o: r.sum_all.at[place1], lambda h: r.sum_all.at[place1], peer1, place1
     )
     start(handed)
-    each(backward, chunks * 3 // 4, chunks)
+    each(backward, chunks * 5 // 8, chunks)
     finish_sum(2)
     for place in range(TEAM):
         strip, side = place // 2, place % 2
@@ -584,6 +582,8 @@
     for part in range(3):
         r.short_out[part] = r.short_all[7 * part : 7 * part + 7]
 
+    for stage in range(3):
+        take(r.sum_first.at[1:TEAM], r.sum_send.at[stage])
     take(r.tail_out, r.send_sem.at[0])
     take(r.edges.at[:, TAIL_ROWS // 16 : 8], r.send_sem.at[1])
     take(r.mixed.at[:, 0:HALF], r.send_sem.at[2])

time: 65.9 us -> 65.9 us (level)
  no operation moved by 1% of the time
where the time goes in v7:
time: 65.9 us; the launch traced here: 65.8 us
  Pallas kernels  62.2 us (94%)
  local copies, waits for them, and re-layouts  2.91 us (4%)
  between operations  0.66 us (1%)
    pallas_call x1, Pallas kernels, shards(): pl.pallas_call(functools.partial(kernel, OPERANDS + RESULTS + list(space)...  62.2 us
    unnamed x7, local copies, waits for them, and re-layouts  2.91 us

profile of v7, /device:TPU:1, one launch (start us, length us, event | category | flops | bytes accessed | tf_op | source)
XLA Modules:
  0.0 65.8 jit_solution(8584421096741237111)
XLA Ops:
  0.6 62.2 %shard_map.85 = (bf16[3,4096,128]{2,1,0:T(8,128)(2,1)S(1)}, f32[3,7,256]{2,1,0:T(8,128)}, f32[64,256]{1,0:T(8,128)}) custom-call(s32[1,2]{1,0:T(1,128)} %bitcast.19, bf16[3,160,4096]{2,1,0:T(8,128)(2,1)} %bitcast.12, f32[3,7,256]{2,1,0:T(8,128)} %bitcast.16, f32[64,256]{1,0:T(8,128)} %bitcast.14, s32[2,128]{1,0:T(2,128)} %bitcast.18, bf16[4096,128]{1,0:T(8,128)(2,1)} %bitcast.13), custom_call_target="tpu_custom_call" | custom-call | tf_op jit(solution)/shard_map/pallas_call | solution.py:606
  62.8 0.0 copy-start.1
  62.8 0.0 copy-start
  62.9 1.7 %copy.12 = bf16[1,3,4096,128]{3,2,1,0:T(8,128)(2,1)} copy(bf16[1,3,4096,128]{3,2,1,0:T(8,128)(2,1)S(1)} %bitcast.11) | data formatting | bytes 6291456
  64.5 0.0 copy-done.1
  64.5 0.6 copy.13
  65.1 0.0 copy-done
  65.1 0.6 copy.14
Async XLA Ops:
  62.8 1.7 %copy-start.1 = (f32[3,7,256]{2,1,0:T(8,128)S(1)}, f32[3,7,256]{2,1,0:T(8,128)}, u32[]{:S(2)}) copy-start(f32[3,7,256]{2,1,0:T(8,128)} %get-tuple-element.7) | copy-start | bytes 64516
  62.8 2.3 %copy-start = (f32[64,256]{1,0:T(8,128)S(1)}, f32[64,256]{1,0:T(8,128)}, u32[]{:S(2)}) copy-start(f32[64,256]{1,0:T(8,128)} %get-tuple-element.8) | copy-start | bytes 196612
